TPU v7x, 128 devices: a whole 4x4x4 slice. The times are simulated.
128 devices in a mesh: dp: 8 (over z, core), seq: 16 (over x, y).
Axes of the slice: x: 4, y: 4, z: 4, core: 2. Of those that a mesh axis runs over, the one named last changes fastest.
Arguments:
- queries: bfloat16 [8, 4096, 2048], P('dp', 'seq'), may hold values from -6 to 6, as said below
- keys: bfloat16 [8, 4096, 2048], P('dp', 'seq'), may hold values from -6 to 6
- values: bfloat16 [8, 4096, 2048], P('dp', 'seq'), may hold values from -6 to 6
- weight_out: bfloat16 [2048, 2048], P('dp'), may hold values from -0.125 to 0.125
- cotangent: bfloat16 [8, 4096, 2048], P('dp', 'seq'), may hold values from -6 to 6
- hidden_mask: int32 [8, 4096], P('dp', 'seq'), may hold values 0 or 1
- pattern: int32 [16, 32, 16], replicated, may hold values from 0 to 31, as said below
- live_slots: int32 [16, 32], replicated, may hold values from 1 to 16, as said below
Outputs:
- block_out: bfloat16 [8, 4096, 2048], P('dp', 'seq')
- grad_queries: bfloat16 [8, 4096, 2048], P('dp', 'seq')
- grad_keys: bfloat16 [8, 4096, 2048], P('dp', 'seq')
- grad_values: bfloat16 [8, 4096, 2048], P('dp', 'seq')
- weight_grad: float32 [2048, 2048], P('seq', 'dp')
Inputs may be any that keep to these rules, and one draw needn't show every extreme that they name: `queries`: queries and keys lie within the range. pattern[h, b] holds 16 distinct block numbers; slot 0 is b itself. Slots 0 to live_slots[h, b] - 1 of pattern[h, b] are used; every head has a query block with all 16 used.
All inputs are finite; a program needn't handle non-finite values. No bound on the sum of `hidden_mask` on one device may be relied on, other than what follows from the above.
Results may differ from a plain program's by a relative error of at most 0.0098.
Values may be sent and summed in bfloat16 or wider, within the bound.
A program may use at most 128 MiB of HBM per device.

v0:
```python
import math

import jax
import jax.numpy as jnp
from jax import lax
from jax.sharding import PartitionSpec as P

H = 16
HD = 128
BLOCK = 128
KMAX = 16


def selector(pat_group, blocks):
    column = jnp.arange(blocks, dtype=jnp.int32)
    return (pat_group[..., None] == column).astype(jnp.bfloat16)


def pick_blocks(onehot, flat_blocks):
    groups, slots, blocks = onehot.shape
    picked = jnp.dot(
        onehot.reshape(groups * slots, blocks), flat_blocks, preferred_element_type=jnp.float32
    )
    return picked.astype(jnp.bfloat16).reshape(groups, slots * BLOCK, HD)


def add_blocks(total, onehot, parts):
    groups, slots, blocks = onehot.shape
    table = onehot.reshape(groups * slots, blocks).astype(jnp.float32)
    flat_parts = parts.reshape(groups * slots, BLOCK * HD)
    return total + lax.dot_general(
        table,
        flat_parts,
        (((0,), (0,)), ((), ())),
        precision=lax.Precision.HIGHEST,
        preferred_element_type=jnp.float32,
    )


def group_scores(q_group, k_flat, onehot, live_group):
    scale = 1.0 / math.sqrt(HD)
    k_group = pick_blocks(onehot, k_flat)
    scores = (
        jnp.einsum("bid,bjd->bij", q_group, k_group, preferred_element_type=jnp.float32) * scale
    )
    slot_of = jnp.arange(KMAX * BLOCK, dtype=jnp.int32) // BLOCK
    valid = slot_of[None, :] < live_group[:, None]
    scores = jnp.where(valid[:, None, :], scores, jnp.float32(-1e30))
    return (scores, k_group)


def layout(length):
    blocks = length // BLOCK
    group = min(blocks, max(1, 512 // BLOCK))
    return (blocks, group, blocks // group)


def forward_head(q_head, k_head, v_head, pat, live):
    length = q_head.shape[0]
    blocks, group, turns = layout(length)
    k_flat = k_head.reshape(blocks, BLOCK * HD)
    v_flat = v_head.reshape(blocks, BLOCK * HD)

    def forward_one_group(args):
        q_group, pat_group, live_group = args
        onehot = selector(pat_group, blocks)
        scores, k_group = group_scores(q_group, k_flat, onehot, live_group)
        v_group = pick_blocks(onehot, v_flat)
        row_max = jnp.max(scores, axis=-1)
        expo = jnp.exp(scores - row_max[..., None])
        row_sum = jnp.sum(expo, axis=-1)
        probs = (expo / row_sum[..., None]).astype(jnp.bfloat16)
        attn = jnp.einsum(
            "bij,bjd->bid", probs, v_group, preferred_element_type=jnp.float32
        ).astype(jnp.bfloat16)
        return (attn, row_max + jnp.log(row_sum))

    attn, row_lse = lax.map(
        forward_one_group,
        (
            q_head.reshape(turns, group, BLOCK, HD),
            pat.reshape(turns, group, KMAX),
            live.reshape(turns, group),
        ),
    )
    return (attn.reshape(length, HD), row_lse.reshape(length))


def backward_head(q_head, k_head, v_head, pat, live, attn, grad_attn, row_lse):
    scale = 1.0 / math.sqrt(HD)
    length = q_head.shape[0]
    blocks, group, turns = layout(length)
    k_flat = k_head.reshape(blocks, BLOCK * HD)
    v_flat = v_head.reshape(blocks, BLOCK * HD)

    def backward_one_group(carry, args):
        acc_k, acc_v = carry
        q_group, pat_group, live_group, a_group, d_group, lse_group = args
        onehot = selector(pat_group, blocks)
        scores, k_group = group_scores(q_group, k_flat, onehot, live_group)
        v_group = pick_blocks(onehot, v_flat)
        back_probs = jnp.exp(scores - lse_group[..., None])
        delta = jnp.sum(d_group.astype(jnp.float32) * a_group.astype(jnp.float32), axis=-1)
        dprobs = jnp.einsum("bid,bjd->bij", d_group, v_group, preferred_element_type=jnp.float32)
        dscores = (back_probs * (dprobs - delta[..., None]) * scale).astype(jnp.bfloat16)
        probs_b = back_probs.astype(jnp.bfloat16)
        grad_q = jnp.einsum(
            "bij,bjd->bid", dscores, k_group, preferred_element_type=jnp.float32
        ).astype(jnp.bfloat16)
        dk_parts = jnp.einsum("bij,bid->bjd", dscores, q_group, preferred_element_type=jnp.float32)
        dv_parts = jnp.einsum("bij,bid->bjd", probs_b, d_group, preferred_element_type=jnp.float32)
        acc_k = add_blocks(acc_k, onehot, dk_parts)
        acc_v = add_blocks(acc_v, onehot, dv_parts)
        return ((acc_k, acc_v), grad_q)

    empty = jnp.zeros((blocks, BLOCK * HD), jnp.float32)
    inputs = (
        q_head.reshape(turns, group, BLOCK, HD),
        pat.reshape(turns, group, KMAX),
        live.reshape(turns, group),
        attn.reshape(turns, group, BLOCK, HD),
        grad_attn.reshape(turns, group, BLOCK, HD),
        row_lse.reshape(turns, group, BLOCK),
    )
    (acc_k, acc_v), grad_q = lax.scan(backward_one_group, (empty, empty), inputs)
    return (
        grad_q.reshape(length, HD),
        acc_k.astype(jnp.bfloat16).reshape(length, HD),
        acc_v.astype(jnp.bfloat16).reshape(length, HD),
    )


def to_heads(x, per_dev):
    length = x.shape[1]
    return x[0].reshape(length, per_dev, HD).transpose(1, 0, 2)


def from_heads(x):
    per_dev, length = (x.shape[0], x.shape[1])
    return x.transpose(1, 0, 2).reshape(1, length, per_dev * HD)


def local(queries, keys, values, weight_out, cotangent, hidden_mask, pattern, live_slots):
    per_dev = H // lax.axis_size("seq")
    first = lax.axis_index("seq") * per_dev
    pat_local = lax.dynamic_slice_in_dim(pattern, first, per_dev, 0)
    live_local = lax.dynamic_slice_in_dim(live_slots, first, per_dev, 0)
    head_q, head_k, head_v = (
        lax.all_to_all(queries, "seq", split_axis=2, concat_axis=1, tiled=True),
        lax.all_to_all(keys, "seq", split_axis=2, concat_axis=1, tiled=True),
        lax.all_to_all(values, "seq", split_axis=2, concat_axis=1, tiled=True),
    )
    length = head_q.shape[1]
    q_split = to_heads(head_q, per_dev)
    k_split = to_heads(head_k, per_dev)
    v_split = to_heads(head_v, per_dev)
    attn_split, lse_split = jax.vmap(forward_head)(q_split, k_split, v_split, pat_local, live_local)
    attn_cat = from_heads(attn_split)
    attn_rows = lax.all_to_all(attn_cat, "seq", split_axis=1, concat_axis=2, tiled=True)
    whole_weight = lax.all_gather(weight_out, "dp", axis=0, tiled=True)
    block_out = jnp.dot(attn_rows[0], whole_weight, preferred_element_type=jnp.float32).astype(
        jnp.bfloat16
    )[None]
    masked = cotangent * hidden_mask[..., None].astype(jnp.bfloat16)
    grad_rows = lax.dot_general(
        masked[0], whole_weight, (((1,), (1,)), ((), ())), preferred_element_type=jnp.float32
    ).astype(jnp.bfloat16)
    grad_cat = lax.all_to_all(grad_rows[None], "seq", split_axis=2, concat_axis=1, tiled=True)
    columns = attn_rows[0]
    summed = lax.psum_scatter(
        lax.dot_general(
            columns, masked[0], (((0,), (0,)), ((), ())), preferred_element_type=jnp.float32
        ),
        "seq",
        scatter_dimension=0,
        tiled=True,
    )
    factor = 1.0 / math.sqrt(lax.axis_size("dp") * length)
    weight_grad = lax.psum_scatter(summed, "dp", scatter_dimension=1, tiled=True) * factor
    grad_split = to_heads(grad_cat, per_dev)
    grad_q, grad_k, grad_v = jax.vmap(backward_head)(
        q_split, k_split, v_split, pat_local, live_local, attn_split, grad_split, lse_split
    )
    out_q, out_k, out_v = (
        lax.all_to_all(from_heads(grad_q), "seq", split_axis=1, concat_axis=2, tiled=True),
        lax.all_to_all(from_heads(grad_k), "seq", split_axis=1, concat_axis=2, tiled=True),
        lax.all_to_all(from_heads(grad_v), "seq", split_axis=1, concat_axis=2, tiled=True),
    )
    return (block_out, out_q, out_k, out_v, weight_grad)


def solution(mesh):
    placed = (
        P("dp", "seq", None),
        P("dp", "seq", None),
        P("dp", "seq", None),
        P("dp", None),
        P("dp", "seq", None),
        P("dp", "seq"),
        P(),
        P(),
    )
    return jax.shard_map(
        local,
        mesh=mesh,
        in_specs=placed,
        out_specs=(
            P("dp", "seq", None),
            P("dp", "seq", None),
            P("dp", "seq", None),
            P("dp", "seq", None),
            P("seq", "dp"),
        ),
        check_vma=False,
    )
```

profile of v0, /device:TPU:34, one launch (start us, length us, event | category | flops | bytes accessed | tf_op | source)
XLA Modules:
  0.0 857.5 jit_solution(1963328386086231533)
XLA Ops:
  13.2 10.6 %reduce.21 = bf16[2048,256]{1,0:T(8,128)(2,1)S(1)} reduce(bf16[2048,1,256]{2,1,0:T(2,128)(2,1)S(1)} %bitcast.200, bf16[]{:T(256)} %broadcast.288), dimensions={1}, to_apply=%bitcast.102.reduce_sub_computation | reduce | bytes 2097154
  24.9 7.5 all-to-all-start
  37.0 11.5 %reduce.22 = bf16[2048,256]{1,0:T(8,128)(2,1)} reduce(bf16[2048,1,256]{2,1,0:T(2,128)(2,1)S(1)} %bitcast.205, bf16[]{:T(256)} %broadcast.288), dimensions={1}, to_apply=%bitcast.104.reduce_sub_computation | reduce | bytes 2097154
  50.6 7.2 all-to-all-start.1
  62.5 11.5 %reduce.23 = bf16[2048,256]{1,0:T(8,128)(2,1)} reduce(bf16[2048,1,256]{2,1,0:T(2,128)(2,1)S(1)} %bitcast.206, bf16[]{:T(256)} %broadcast.288), dimensions={1}, to_apply=%bitcast.106.reduce_sub_computation | reduce | bytes 2097154
  76.1 7.2 all-to-all-start.2
  107.3 144.6 %while.31 = (s32[]{:T(128)}, bf16[8,1,4,128,128]{4,3,2,1,0:T(8,128)(2,1)}, f32[8,1,4,128]{3,2,1,0:T(4,128)S(1)}, s32[8,1,4]{2,1,0:T(1,128)S(1)}, bf16[8,1,4,128,...) while((s32[]{:T(128)}, ...), condition=%wide.region_3.4_spmd, body=%wide.region_0.3_spmd.sunk | while | flops 685862400 | bytes 40175300 | solution.py:78
  255.1 23.7 %reduce.24 = bf16[4096,128]{1,0:T(8,128)(2,1)} reduce(bf16[4096,1,128]{2,1,0:T(2,128)(2,1)S(1)} %bitcast.207, bf16[]{:T(256)} %broadcast.288), dimensions={1}, to_apply=%bitcast.136.reduce_sub_computation | reduce | bytes 2097154
  281.0 6.0 all-to-all-start.3
  287.1 6.8 fusion.50
  298.4 11.5 %reduce.25 = bf16[2048,256]{1,0:T(8,128)(2,1)} reduce(bf16[2048,1,256]{2,1,0:T(2,128)(2,1)S(1)} %bitcast.202, bf16[]{:T(256)} %broadcast.288), dimensions={1}, to_apply=%bitcast.110.reduce_sub_computation | reduce | bytes 2097154
  312.2 7.3 all-to-all-start.4
  326.6 8.1 fusion.51
  343.8 377.3 %while.32 = (s32[]{:T(128)}, f32[1,32,16384]{2,1,0:T(8,128)}, f32[1,32,16384]{2,1,0:T(8,128)}, bf16[8,1,4,128,128]{4,3,2,1,0:T(8,128)(2,1)}, s32[8,1,4,16]{3,2,1...) while((s32[]{:T(128)}, f32[1,32,16384]{2,1,0:T(8,128)}, ...), condition=%wide.region_6.7_spmd.clone, body=%wide.region_4.6_spmd.clone.sunk | while | flops 2294644224 | bytes 124694904 | solution.py:125
  365.3 5.2 reshape.481
  370.4 5.3 fusion.125
  379.5 5.4 reshape.480
  384.9 5.1 fusion.123
  412.6 5.0 reshape.481
  417.6 5.9 fusion.125
  427.2 5.1 reshape.480
  432.3 5.1 fusion.123
  464.8 5.9 fusion.125
  474.4 5.1 reshape.480
  479.5 5.1 fusion.123
  506.8 4.9 reshape.481
  511.8 5.9 fusion.125
  521.4 5.1 reshape.480
  526.5 5.1 fusion.123
  558.8 5.9 fusion.125
  568.5 5.1 reshape.480
  573.6 5.1 fusion.123
  605.9 5.9 fusion.125
  615.5 5.1 reshape.480
  620.6 5.1 fusion.123
  652.9 5.9 fusion.125
  662.6 5.1 reshape.480
  667.6 5.1 fusion.123
  699.9 5.9 fusion.125
  709.6 5.1 reshape.480
  714.7 5.1 fusion.123
  724.3 22.6 %reduce.26 = bf16[4096,128]{1,0:T(8,128)(2,1)S(1)} reduce(bf16[4096,1,128]{2,1,0:T(2,128)(2,1)S(1)} %bitcast.203, bf16[]{:T(256)} %broadcast.288), dimensions={1}, to_apply=%bitcast.135.reduce_sub_computation | reduce | bytes 2097154
  747.9 7.4 all-to-all-start.5
  757.9 22.4 %reduce.27 = bf16[4096,128]{1,0:T(8,128)(2,1)S(1)} reduce(bf16[4096,1,128]{2,1,0:T(2,128)(2,1)S(1)} %bitcast.204, bf16[]{:T(256)} %broadcast.288), dimensions={1}, to_apply=%bitcast.114.reduce_sub_computation | reduce | bytes 2097154
  781.3 7.6 all-to-all-start.6
  790.7 22.4 %reduce.28 = bf16[4096,128]{1,0:T(8,128)(2,1)S(1)} reduce(bf16[4096,1,128]{2,1,0:T(2,128)(2,1)S(1)} %bitcast.201, bf16[]{:T(256)} %broadcast.288), dimensions={1}, to_apply=%bitcast.116.reduce_sub_computation | reduce | bytes 2097154
  814.2 7.2 all-to-all-start.7
  821.5 6.7 fusion.49
  (427 shorter events, 481.0 us)
Async XLA Ops:
  8.0 76.9 %copy-start = (s32[16,32,16]{1,2,0:T(8,128)S(1)}, s32[16,32,16]{1,2,0:T(8,128)}, u32[]{:S(2)}) copy-start(s32[16,32,16]{1,2,0:T(8,128)} %param.18) | copy-start | bytes 98308
  24.9 25.8 %all-to-all-start = ((bf16[16,2,16384]{2,1,0:T(2,128)(2,1)}), bf16[16,2,16384]{2,1,0:T(2,128)(2,1)S(1)}, u32[]{:S(2)}, u32[]{:S(2)}) async-start(bf16[16,2,16384]{2,1,0:T(2,128)(2,1)} %reshape.454), calls=%async_computation | async-start | bytes 2097152 | tf_op jit(solution)/shard_map/all_to_all | solution.py:149
  50.6 25.5 %all-to-all-start.1 = ((bf16[16,2,16384]{2,1,0:T(2,128)(2,1)}), bf16[16,2,16384]{2,1,0:T(2,128)(2,1)}, u32[]{:S(2)}, u32[]{:S(2)}) async-start(bf16[16,2,16384]{2,1,0:T(2,128)(2,1)} %reshape.456), calls=%async_computation.1 | async-start | bytes 2097152 | tf_op jit(solution)/shard_map/all_to_all | solution.py:150
  76.1 21.4 %all-to-all-start.2 = ((bf16[16,2,16384]{2,1,0:T(2,128)(2,1)}), bf16[16,2,16384]{2,1,0:T(2,128)(2,1)}, u32[]{:S(2)}, u32[]{:S(2)}) async-start(bf16[16,2,16384]{2,1,0:T(2,128)(2,1)} %reshape.458), calls=%async_computation.2 | async-start | bytes 2097152 | tf_op jit(solution)/shard_map/all_to_all | solution.py:151
  83.4 203.7 %all-gather.2.cloned.1.call-start = ((), (), s32[]{:S(2)}) async-start(), calls=%async_computation.10 | async-start | bytes 9437184 | tf_op jit(solution)/shard_map/all_gather | solution.py:160
  121.8 1.6 copy-start.9
  194.1 1.6 copy-start.9
  212.1 1.6 copy-start.9
  230.2 1.6 copy-start.9
  248.3 1.6 copy-start.9
  278.8 8.2 copy-start.14
  278.8 8.3 copy-start.12
  281.0 31.2 %all-to-all-start.3 = ((bf16[16,2,16384]{2,1,0:T(2,128)(2,1)}), bf16[16,2,16384]{2,1,0:T(2,128)(2,1)}, u32[]{:S(2)}, u32[]{:S(2)}) async-start(bf16[16,2,16384]{2,1,0:T(2,128)(2,1)} %reshape.460), calls=%async_computation.3 | async-start | bytes 2097152 | tf_op jit(solution)/shard_map/all_to_all | solution.py:159
  312.2 22.5 %all-to-all-start.4 = ((bf16[16,2,16384]{2,1,0:T(2,128)(2,1)}), bf16[16,2,16384]{2,1,0:T(2,128)(2,1)}, u32[]{:S(2)}, u32[]{:S(2)}) async-start(bf16[16,2,16384]{2,1,0:T(2,128)(2,1)} %reshape.462), calls=%async_computation.4 | async-start | bytes 2097152 | tf_op jit(solution)/shard_map/all_to_all | solution.py:168
  319.5 436.0 %reduce-scatter.3.cloned.1.call-start = ((), (), s32[]{:S(2)}) async-start(), calls=%async_computation.11 | async-start | bytes 17825792 | tf_op jit(solution)/shard_map/reduce_scatter | solution.py:170
  326.5 8.2 copy-start.10
  356.2 2.2 copy-start.4
  358.4 1.8 copy-start.3
  379.5 5.4 copy-start.6
  403.6 2.2 copy-start.4
  405.7 1.8 copy-start.3
  427.2 5.1 copy-start.6
  450.8 2.1 copy-start.4
  452.9 1.8 copy-start.3
  474.4 5.1 copy-start.6
  497.8 2.1 copy-start.4
  500.0 1.8 copy-start.3
  521.4 5.1 copy-start.6
  544.9 2.1 copy-start.4
  547.0 1.8 copy-start.3
  568.5 5.1 copy-start.6
  591.9 2.1 copy-start.4
  594.0 1.8 copy-start.3
  615.5 5.1 copy-start.6
  638.9 2.1 copy-start.4
  641.1 1.8 copy-start.3
  662.6 5.1 copy-start.6
  686.0 2.1 copy-start.4
  688.1 1.8 copy-start.3
  709.6 5.1 copy-start.6
  747.9 8.2 copy-start.8
  747.9 33.4 %all-to-all-start.5 = ((bf16[16,2,16384]{2,1,0:T(2,128)(2,1)}), bf16[16,2,16384]{2,1,0:T(2,128)(2,1)}, u32[]{:S(2)}, u32[]{:S(2)}) async-start(bf16[16,2,16384]{2,1,0:T(2,128)(2,1)} %reshape.464), calls=%async_computation.5 | async-start | bytes 2097152 | tf_op jit(solution)/shard_map/all_to_all | solution.py:185
  755.4 92.6 %reduce-scatter.5.cloned.1.call-start = ((), (), s32[]{:S(2)}) async-start(), calls=%async_computation.12 | async-start | bytes 1179648 | tf_op jit(solution)/shard_map/reduce_scatter | solution.py:179
  780.2 8.8 %copy-start.5 = (f32[1,32,16384]{2,1,0:T(8,128)S(1)}, f32[1,32,16384]{2,1,0:T(8,128)}, u32[]{:S(2)}) copy-start(f32[1,32,16384]{2,1,0:T(8,128)} %get-tuple-element.264) | copy-start | bytes 6291460
  781.3 32.9 %all-to-all-start.6 = ((bf16[16,2,16384]{2,1,0:T(2,128)(2,1)}), bf16[16,2,16384]{2,1,0:T(2,128)(2,1)}, u32[]{:S(2)}, u32[]{:S(2)}) async-start(bf16[16,2,16384]{2,1,0:T(2,128)(2,1)} %reshape.466), calls=%async_computation.6 | async-start | bytes 2097152 | tf_op jit(solution)/shard_map/all_to_all | solution.py:186
  813.1 8.4 copy-start.11
  814.2 30.6 %all-to-all-start.7 = ((bf16[16,2,16384]{2,1,0:T(2,128)(2,1)}), bf16[16,2,16384]{2,1,0:T(2,128)(2,1)S(1)}, u32[]{:S(2)}, u32[]{:S(2)}) async-start(bf16[16,2,16384]{2,1,0:T(2,128)(2,1)} %reshape.468), calls=%async_computation.7 | async-start | bytes 2097152 | tf_op jit(solution)/shard_map/all_to_all | solution.py:187
  846.0 3.6 copy-start.1
  (20 other events, 27.3 us)
Sparse Core Ops, SparseCore 0:
  85.9 50.7 all-gather.1
  758.6 30.3 reduce-scatter.4
Sparse Core Ops, SparseCore 1:
  334.8 111.9 reduce-scatter.2
where the time goes:
time: 871 us; the launch traced here: 857 us
  matrix products  317 us (36%)
  local copies, waits for them, and re-layouts  303 us (35%)
  other arithmetic  157 us (18%)
  starting transfers between devices  57.8 us (7%)
  between operations  16.3 us (2%)
    another operation x50, local copies, waits for them, and re-layouts  183 us
    unnamed x10, other arithmetic  136 us
    dot_general x16, matrix products, add_blocks(): lax.dot_general(table, flat_parts, (((0,), (0,)), ((), ())), precision=la...  87.5 us
    dot_general x32, matrix products, pick_blocks(): jnp.dot(onehot.reshape(groups * slots, blocks), flat_blocks, preferred_el...  75.8 us
    unnamed x49, local copies, waits for them, and re-layouts  66.1 us
    dot_general x16, matrix products, group_scores(): jnp.einsum('bid,bjd->bij', q_group, k_group, preferred_element_type=jnp.f...  31.1 us
    dot_general x8, matrix products, backward_one_group(): jnp.einsum('bij,bid->bjd', dscores, q_group, preferred_element_type=jnp.f...  29.8 us
    dot_general x8, matrix products, backward_one_group(): jnp.einsum('bij,bid->bjd', probs_b, d_group, preferred_element_type=jnp.f...  29.8 us
  transfers between devices with their start and end apart: 11, of which 1 were waited for; matrix products, arithmetic and copies ran while one was open for 85% of the time, Pallas kernels for 0%

commit v1 on v0

v1 whole, which is shorter than its diff:
```python
import functools
import math

import jax
import jax.numpy as jnp
from jax import lax
from jax.experimental import pallas as pl
from jax.experimental.pallas import tpu as pltpu
from jax.sharding import PartitionSpec as P

HD = 128
BLOCK = 128
KMAX = 16
STEP = 4
SCALE = 1.0 / math.sqrt(HD)
BF = jnp.bfloat16
MESH = pl.DeviceIdType.MESH
NT = (((1,), (1,)), ((), ()))


def columns(index, width):
    return pl.ds(pl.multiple_of(index * width, width), width)


def greet(dp, seq, ndp, nseq):
    barrier = pltpu.get_barrier_semaphore()

    @pl.loop(1, nseq)
    def _(step):
        pl.semaphore_signal(barrier, inc=1, device_id=(dp, lax.rem(seq + step, nseq)), device_id_type=MESH)

    @pl.loop(1, ndp)
    def _(step):
        pl.semaphore_signal(barrier, inc=1, device_id=(lax.rem(dp + step, ndp), seq), device_id_type=MESH)

    pl.semaphore_wait(barrier, nseq + ndp - 2)


class Ring:
    def __init__(self, part, buf, dp, seq, ndp, send, recv, give, take):
        self.part, self.buf, self.dp, self.seq = part, buf, dp, seq
        self.chips = ndp // 2
        self.z, self.core = dp // 2, lax.rem(dp, 2)
        self.send, self.recv, self.give, self.take = send, recv, give, take

    def slot(self, offset, other=False):
        core = 1 - self.core if other else self.core
        return lax.rem(self.z + self.chips + offset, self.chips) * 2 + core

    def half(self, slot, half):
        return self.part(self.buf.at[slot], half)

    def hop(self, index, source=None):
        up = index % 2 == 0
        half = (0, 1, 1, 0, 0, 1)[index]
        slot = self.slot(0) if index < 4 else self.slot(-1 if up else 1)
        target = self.slot(1 if up else -1)
        src = self.half(slot, half) if source is None else self.part(source, half)
        return pltpu.make_async_remote_copy(src, self.half(slot, half), self.send.at[index], self.recv.at[index],
                                            device_id=(target, self.seq), device_id_type=MESH)

    def hand(self, index, source=None):
        if index < 2:
            slot, half = self.slot(0), index
        else:
            slot = self.slot((-1, 1, -1, 1, 2, 2)[index - 2])
            half = (0, 1, 1, 0, 0, 1)[index - 2]
        src = self.half(slot, half) if source is None else self.part(source, half)
        return pltpu.make_async_remote_copy(src, self.half(slot, half), self.give.at[index], self.take.at[index],
                                            device_id=(self.slot(0, True), self.seq), device_id_type=MESH)

    def start(self, half, source=None):
        for index in ((0, 3), (1, 2))[half]:
            self.hop(index, source).start()
        self.hand(half, source).start()

    def run(self, use):
        use(self.slot(0))
        for index in (0, 1):
            self.hop(index).wait_recv()
            self.hop(index + 4).start()
            self.hand(index + 2).start()
        self.hand(0).wait_recv()
        self.hand(1).wait_recv()
        use(self.slot(0, True))
        for index, offset in ((2, -1), (3, 1)):
            self.hop(index).wait_recv()
            self.hand(index + 2).start()
            use(self.slot(offset))
        for first, second, offset in ((2, 4, -1), (3, 5, 1)):
            self.hand(first).wait_recv()
            self.hand(second).wait_recv()
            use(self.slot(offset, True))
        for index in (4, 5):
            self.hop(index).wait_recv()
            self.hand(index + 2).start()
        use(self.slot(2))
        self.hand(6).wait_recv()
        self.hand(7).wait_recv()
        use(self.slot(2, True))
        for index in range(6):
            self.hop(index).wait_send()
        for index in range(8):
            self.hand(index).wait_send()


def bring(q_ref, k_ref, v_ref, w_ref, m_ref, hq_ref, hk_ref, hv_ref, hd_ref, wf_ref, mc_ref,
          w_buf, m_buf, g_buf, a_send, a_recv, w_send, w_recv, f_send, f_recv, m_send, m_recv, local, keep_w):
    dp, seq = lax.axis_index("dp"), lax.axis_index("seq")
    ndp, nseq = lax.axis_size("dp"), lax.axis_size("seq")
    rows, mine = w_ref.shape[0], q_ref.shape[0]
    tensors = ((q_ref, hq_ref), (k_ref, hk_ref), (v_ref, hv_ref))
    greet(dp, seq, ndp, nseq)

    def row_half(ref, half):
        return ref.at[pl.ds(half * (rows // 2), rows // 2), :]

    ring = Ring(row_half, w_buf, dp, seq, ndp, w_send, w_recv, f_send, f_recv)

    def sides(step):
        other = lax.rem(dp + step, ndp)
        return pltpu.make_async_remote_copy(m_ref.at[:, columns(other, rows)], mc_ref.at[dp], m_send.at[step], m_recv.at[step],
                                            device_id=(other, seq), device_id_type=MESH)

    def spread(which, step):
        src, dst = tensors[which]
        other = lax.rem(seq + step, nseq)
        return pltpu.make_async_remote_copy(src.at[:, columns(other, HD)], dst.at[columns(seq, mine), :],
                                            a_send.at[which, step], a_recv.at[which, step], device_id=(dp, other), device_id_type=MESH)

    def keep(which):
        src, dst = tensors[which]
        return pltpu.make_async_copy(src.at[:, columns(seq, HD)], dst.at[columns(seq, mine), :], local.at[which])

    own_w = pltpu.make_async_copy(w_ref, w_buf.at[dp], local.at[3])
    own_m = pltpu.make_async_copy(m_ref, m_buf, local.at[4])
    own_c = pltpu.make_async_copy(m_ref.at[:, columns(dp, rows)], mc_ref.at[dp], local.at[5])
    own_w.start()
    own_m.start()
    ring.start(0, w_ref)
    ring.start(1, w_ref)
    for which in range(3):
        @pl.loop(1, nseq)
        def _(step):
            spread(which, step).start()
        keep(which).start()
    own_c.start()

    @pl.loop(1, ndp)
    def _(step):
        sides(step).start()

    own_m.wait()

    def store(slot):
        return pltpu.make_async_copy(w_buf.at[slot], wf_ref.at[slot], keep_w.at[slot])

    def give(head, source):
        return pltpu.make_async_remote_copy(g_buf.at[:, columns(head, HD)], hd_ref.at[columns(source, mine), :],
                                            a_send.at[3, head], a_recv.at[3, source], device_id=(dp, head), device_id_type=MESH)

    def own_g():
        return pltpu.make_async_copy(g_buf.at[:, columns(seq, HD)], hd_ref.at[columns(seq, mine), :], local.at[6])

    def use(slot):
        store(slot).start()
        g_buf[:, columns(slot, rows)] = lax.dot_general(m_buf[...], w_buf[slot], NT, preferred_element_type=jnp.float32).astype(BF)
        for half in range(rows // HD):
            head = slot * (rows // HD) + half

            @pl.when(head != seq)
            def _():
                give(head, seq).start()

            @pl.when(head == seq)
            def _():
                own_g().start()

    own_w.wait()
    ring.run(use)
    own_c.wait()

    @pl.loop(1, ndp)
    def _(step):
        sides(step).wait()

    @pl.loop(0, ndp)
    def _(slot):
        store(slot).wait()

    for which in range(3):
        @pl.loop(1, nseq)
        def _(step):
            spread(which, step).wait()
        keep(which).wait()

    own_g().wait()

    @pl.loop(0, nseq)
    def _(other):
        @pl.when(other != seq)
        def _():
            give(other, seq).wait_send()
            give(other, other).wait_recv()


def bring_in(q, k, v, w, m):
    ndp, nseq = lax.axis_size("dp"), lax.axis_size("seq")
    mine, width = q.shape
    rows = w.shape[0]
    place = pl.BlockSpec(memory_space=pl.ANY)
    head = jax.ShapeDtypeStruct((mine * nseq, HD), BF)
    dma = pltpu.SemaphoreType.DMA
    return pl.pallas_call(
        bring,
        out_shape=(head,) * 4 + (jax.ShapeDtypeStruct((ndp, rows, width), BF), jax.ShapeDtypeStruct((ndp, mine, rows), BF)),
        in_specs=[place] * 5,
        out_specs=(place,) * 6,
        scratch_shapes=[
            pltpu.VMEM((ndp, rows, width), BF), pltpu.VMEM((mine, width), BF), pltpu.VMEM((mine, width), BF),
            dma((4, nseq)), dma((4, nseq)), dma((6,)), dma((6,)), dma((8,)), dma((8,)), dma((ndp,)), dma((ndp,)), dma((7,)), dma((ndp,))],
        compiler_params=pltpu.CompilerParams(collective_id=0, has_side_effects=True, vmem_limit_bytes=40 * 2**20),
        name="bring_in",
    )(q, k, v, w, m)


def take(factor, o_ref, dq_ref, dk_ref, dv_ref, wf_ref, mc_ref, out_ref, oq_ref, ok_ref, ov_ref, wg_ref,
         a_buf, w_buf, c_buf, ct_buf, sum_buf, p_buf, part_buf, out_buf, wg_buf,
         o_send, o_recv, g_send, g_recv, r_send, r_recv, f_send, f_recv, p_send, p_recv, local):
    dp, seq = lax.axis_index("dp"), lax.axis_index("seq")
    ndp, nseq = lax.axis_size("dp"), lax.axis_size("seq")
    mine, width = a_buf.shape[1:]
    rows = width // ndp
    tensors = ((dq_ref, oq_ref), (dk_ref, ok_ref), (dv_ref, ov_ref))
    greet(dp, seq, ndp, nseq)

    def column_half(ref, half):
        return ref.at[:, pl.ds(half * (width // 2), width // 2)]

    ring = Ring(column_half, a_buf, dp, seq, ndp, r_send, r_recv, f_send, f_recv)

    def home(other, source):
        return pltpu.make_async_remote_copy(o_ref.at[columns(other, mine), :], a_buf.at[dp].at[:, columns(source, HD)],
                                            o_send.at[other], o_recv.at[source], device_id=(dp, other), device_id_type=MESH)

    def spread(which, step):
        src, dst = tensors[which]
        other = lax.rem(seq + step, nseq)
        return pltpu.make_async_remote_copy(src.at[columns(other, mine), :], dst.at[:, columns(seq, HD)],
                                            g_send.at[which, step], g_recv.at[which, step], device_id=(dp, other), device_id_type=MESH)

    def keep(which):
        src, dst = tensors[which]
        return pltpu.make_async_copy(src.at[columns(seq, mine), :], dst.at[:, columns(seq, HD)], local.at[which])

    own_o = pltpu.make_async_copy(o_ref.at[columns(seq, mine), :], a_buf.at[dp].at[:, columns(seq, HD)], local.at[3])
    own_c = pltpu.make_async_copy(mc_ref, c_buf, local.at[4])
    own_w = pltpu.make_async_copy(wf_ref, w_buf, local.at[5])

    @pl.loop(1, nseq)
    def _(step):
        home(lax.rem(seq + step, nseq), seq).start()

    own_o.start()
    own_c.start()
    own_w.start()
    for which in range(3):
        @pl.loop(1, nseq)
        def _(step):
            spread(which, step).start()
        keep(which).start()

    own_c.wait()
    for slot in range(ndp):
        ct_buf[slot] = c_buf[slot].T
    sum_buf[...] = jnp.zeros_like(sum_buf)
    own_o.wait()
    for half in range(2):
        @pl.loop(half * (nseq // 2), (half + 1) * (nseq // 2))
        def _(other):
            @pl.when(other != seq)
            def _():
                home(other, other).wait_recv()
        ring.start(half)

    own_w.wait()

    @pl.loop(0, ndp)
    def _(tile):
        at = columns(tile, rows)
        total = jnp.zeros((mine, rows), jnp.float32)
        for slot in range(ndp):
            total += jnp.dot(a_buf[dp, :, slot * rows:(slot + 1) * rows], w_buf[slot, :, at], preferred_element_type=jnp.float32)
        out_buf[:, at] = total.astype(BF)

    own_out = pltpu.make_async_copy(out_buf, out_ref, local.at[6])
    own_out.start()

    def use(slot):
        @pl.loop(0, ndp)
        def _(tile):
            at = columns(tile, rows)
            sum_buf[:, at] += jnp.dot(ct_buf[slot], a_buf[slot, :, at], preferred_element_type=jnp.float32)

    ring.run(use)
    p_buf[...] = sum_buf[...].astype(BF)

    def share(head, source):
        return pltpu.make_async_remote_copy(p_buf.at[:, columns(head, HD)], part_buf.at[source],
                                            p_send.at[head], p_recv.at[source], device_id=(dp, head), device_id_type=MESH)

    own_p = pltpu.make_async_copy(p_buf.at[:, columns(seq, HD)], part_buf.at[seq], local.at[7])

    @pl.loop(1, nseq)
    def _(step):
        share(lax.rem(seq + step, nseq), seq).start()

    own_p.start()
    own_out.wait()
    for which in range(3):
        @pl.loop(1, nseq)
        def _(step):
            spread(which, step).wait()
        keep(which).wait()

    own_p.wait()

    @pl.loop(0, nseq)
    def _(other):
        @pl.when(other != seq)
        def _():
            home(other, seq).wait_send()
            share(other, seq).wait_send()
            share(other, other).wait_recv()

    total = part_buf[0].astype(jnp.float32)
    for source in range(1, nseq):
        total += part_buf[source].astype(jnp.float32)
    wg_buf[...] = total.T * factor
    last = pltpu.make_async_copy(wg_buf, wg_ref, local.at[8])
    last.start()
    last.wait()


def take_home(o, dq, dk, dv, wf, mc):
    ndp, nseq = lax.axis_size("dp"), lax.axis_size("seq")
    mine, rows = mc.shape[1:]
    width = rows * ndp
    place = pl.BlockSpec(memory_space=pl.ANY)
    out = jax.ShapeDtypeStruct((mine, width), BF)
    dma = pltpu.SemaphoreType.DMA
    factor = 1.0 / math.sqrt(ndp * nseq * mine)
    return pl.pallas_call(
        functools.partial(take, factor),
        out_shape=(out,) * 4 + (jax.ShapeDtypeStruct((HD, rows), jnp.float32),),
        in_specs=[place] * 6,
        out_specs=(place,) * 5,
        scratch_shapes=[
            pltpu.VMEM((ndp, mine, width), BF), pltpu.VMEM((ndp, rows, width), BF), pltpu.VMEM((ndp, mine, rows), BF),
            pltpu.VMEM((ndp, rows, mine), BF), pltpu.VMEM((rows, width), jnp.float32), pltpu.VMEM((rows, width), BF),
            pltpu.VMEM((nseq, rows, HD), BF), pltpu.VMEM((mine, width), BF), pltpu.VMEM((HD, rows), jnp.float32),
            dma((nseq,)), dma((nseq,)), dma((3, nseq)), dma((3, nseq)), dma((6,)), dma((6,)), dma((8,)), dma((8,)),
            dma((nseq,)), dma((nseq,)), dma((9,))],
        compiler_params=pltpu.CompilerParams(collective_id=1, has_side_effects=True, vmem_limit_bytes=48 * 2**20),
        name="take_home",
    )(o, dq, dk, dv, wf, mc)

def attend(step, pat_ref, live_ref, q_ref, k_ref, v_ref, d_ref, o_ref, dq_ref, dk_ref, dv_ref, kt_ref, vt_ref, acc_ref, e_ref, g_ref):
    nb = q_ref.shape[0] // BLOCK
    fold = lambda x: x.reshape(BLOCK // 8, 8, BLOCK)

    @pl.loop(0, nb)
    def _(b):
        rows = pl.ds(pl.multiple_of(b * BLOCK, BLOCK), BLOCK)
        kt_ref[rows, :] = k_ref[rows, :].T
        vt_ref[rows, :] = v_ref[rows, :].T
        acc_ref[rows, :] = jnp.zeros((BLOCK, 2 * HD), jnp.float32)

    def with_slots(count, b):
        rows = pl.ds(pl.multiple_of(b * BLOCK, BLOCK), BLOCK)
        live = live_ref[b]
        q = q_ref[rows, :]
        d = d_ref[rows, :]
        none = jnp.zeros((BLOCK, HD), BF)
        enter = jnp.concatenate([jnp.concatenate([q, none], 1), jnp.concatenate([none, d], 1)], 0)
        leave = jnp.concatenate([jnp.concatenate([d, none], 1), jnp.concatenate([none, q], 1)], 0)
        at = [pl.ds(pl.multiple_of(pat_ref[b * KMAX + j] * BLOCK, BLOCK), BLOCK) for j in range(count)]
        top = jnp.full((8, BLOCK), -1e30, jnp.float32)
        total = jnp.zeros((8, BLOCK), jnp.float32)
        mixed = jnp.zeros((8, BLOCK), jnp.float32)
        tops = []
        for j in range(count):
            both = lax.dot_general(jnp.concatenate([k_ref[at[j], :], v_ref[at[j], :]], 1), enter,
                                   (((1,), (1,)), ((), ())), preferred_element_type=jnp.float32)
            s, g = both[:, :BLOCK], both[:, BLOCK:]
            if j > count - step:
                s = jnp.where(j < live, s, jnp.float32(-1e30))
            new = jnp.maximum(top, jnp.max(fold(s), axis=0))
            old = jnp.exp((top - new) * SCALE)
            e = jnp.exp((fold(s) - new[None]) * SCALE)
            total = total * old + jnp.sum(e, axis=0)
            mixed = mixed * old + jnp.sum(e * fold(g), axis=0)
            e_ref[j * BLOCK:(j + 1) * BLOCK, :] = e.reshape(BLOCK, BLOCK)
            g_ref[j * BLOCK:(j + 1) * BLOCK, :] = g
            tops.append(new)
            top = new
        peak = jnp.max(top, axis=0, keepdims=True)
        level = jnp.exp((top - peak) * SCALE)
        inverse = 1.0 / jnp.sum(total * level, axis=0, keepdims=True)
        delta = jnp.sum(mixed * level, axis=0, keepdims=True) * inverse
        o_sum = jnp.zeros((HD, BLOCK), jnp.float32)
        q_sum = jnp.zeros((HD, BLOCK), jnp.float32)
        for j in range(0, count, 2):
            probs, slopes = [], []
            for i in (j, j + 1):
                e = e_ref[i * BLOCK:(i + 1) * BLOCK, :]
                g = g_ref[i * BLOCK:(i + 1) * BLOCK, :]
                weight = jnp.exp((tops[i] - peak) * SCALE) * inverse
                p = (fold(e) * weight[None]).reshape(BLOCK, BLOCK)
                pb = p.astype(BF)
                sb = (p * (g - delta)).astype(BF)
                acc_ref[at[i], :] += jnp.dot(jnp.concatenate([pb, sb], 1), leave, preferred_element_type=jnp.float32)
                probs.append(pb)
                slopes.append(sb)
            o_sum += jnp.dot(jnp.concatenate([vt_ref[at[j], :], vt_ref[at[j + 1], :]], 1),
                             jnp.concatenate(probs, 0), preferred_element_type=jnp.float32)
            q_sum += jnp.dot(jnp.concatenate([kt_ref[at[j], :], kt_ref[at[j + 1], :]], 1),
                             jnp.concatenate(slopes, 0), preferred_element_type=jnp.float32)
        o_ref[rows, :] = o_sum.T.astype(BF)
        dq_ref[rows, :] = (q_sum.T * SCALE).astype(BF)

    @pl.loop(0, nb)
    def _(b):
        branches = [functools.partial(with_slots, c) for c in range(step, KMAX + 1, step)]
        lax.switch((live_ref[b] - 1) // step, branches, b)

    @pl.loop(0, nb)
    def _(b):
        rows = pl.ds(pl.multiple_of(b * BLOCK, BLOCK), BLOCK)
        dv_ref[rows, :] = acc_ref[rows, :HD].astype(BF)
        dk_ref[rows, :] = (acc_ref[rows, HD:] * SCALE).astype(BF)


def attention(q, k, v, d, pat, live):
    length = q.shape[0]
    out = jax.ShapeDtypeStruct((length, HD), BF)
    vm = pl.BlockSpec(memory_space=pltpu.VMEM)
    sm = pl.BlockSpec(memory_space=pltpu.SMEM)
    return pl.pallas_call(
        functools.partial(attend, STEP),
        out_shape=(out,) * 4,
        in_specs=[sm, sm, vm, vm, vm, vm],
        out_specs=(vm,) * 4,
        scratch_shapes=[
            pltpu.VMEM((length, HD), BF), pltpu.VMEM((length, HD), BF),
            pltpu.VMEM((length, 2 * HD), jnp.float32),
            pltpu.VMEM((KMAX * BLOCK, BLOCK), jnp.float32), pltpu.VMEM((KMAX * BLOCK, BLOCK), jnp.float32)],
        compiler_params=pltpu.CompilerParams(vmem_limit_bytes=40 * 2**20),
        name="attention",
    )(pat.reshape(-1), live, q, k, v, d)


def local(queries, keys, values, weight_out, cotangent, hidden_mask, pattern, live_slots):
    seq = lax.axis_index("seq")
    pat = lax.dynamic_index_in_dim(pattern, seq, 0, keepdims=False)
    live = lax.dynamic_index_in_dim(live_slots, seq, 0, keepdims=False)
    masked = cotangent[0] * hidden_mask[0][:, None].astype(BF)
    q, k, v, d, weights, sides = bring_in(queries[0], keys[0], values[0], weight_out, masked)
    attn, dq, dk, dv = attention(q, k, v, d, pat, live)
    block_out, dq, dk, dv, weight_grad = take_home(attn, dq, dk, dv, weights, sides)
    return (block_out[None], dq[None], dk[None], dv[None], weight_grad)


def solution(mesh):
    rows = P("dp", "seq", None)
    return jax.shard_map(
        local,
        mesh=mesh,
        in_specs=(rows, rows, rows, P("dp", None), rows, P("dp", "seq"), P(), P()),
        out_specs=(rows, rows, rows, rows, P("seq", "dp")),
        check_vma=False,
    )
```

time: 871 us -> 207 us (0.24)
  the two profiles are of different devices: /device:TPU:34 before, /device:TPU:1 now
where the time goes in v1:
time: 207 us; the launch traced here: 204 us
  Pallas kernels  187 us (90%)
  local copies, waits for them, and re-layouts  14.2 us (7%)
  other arithmetic  2.1 us (1%)
    pallas_call x1, Pallas kernels, take_home(): pl.pallas_call(functools.partial(take, factor), out_shape=(out,) * 4 + (j...  84.2 us
    pallas_call x1, Pallas kernels, bring_in(): pl.pallas_call(bring, out_shape=(head,) * 4 + (jax.ShapeDtypeStruct((ndp,...  65.1 us
    pallas_call x1, Pallas kernels, attention(): pl.pallas_call(functools.partial(attend, STEP), out_shape=(out,) * 4, in_...  37.7 us
    unnamed x23, local copies, waits for them, and re-layouts  13.3 us

profile of v1, /device:TPU:1, one launch (start us, length us, event | category | flops | bytes accessed | tf_op | source)
XLA Modules:
  0.0 203.9 jit_solution(14716825867931875762)
XLA Ops:
  0.6 0.0 copy-start
  0.7 0.7 convert_reduce_fusion
  1.4 0.7 dynamic-slice_bitcast_fusion.live_ref
  2.1 0.0 copy-done
  2.1 0.1 copy.13
  2.2 0.1 reshape.22.pat_ref
  2.2 1.4 bitcast_multiply_fusion.m_ref
  3.6 0.0 copy-start.1
  3.6 1.2 copy-done.1
  4.8 0.0 copy-start.2
  4.8 1.2 copy-done.2
  6.1 0.0 copy-start.3
  6.1 1.2 copy-done.3
  7.3 0.0 copy-start.4
  7.3 1.2 copy-done.4
  8.5 65.1 %bring_in.1 = (bf16[4096,128]{1,0:T(8,128)(2,1)S(1)}, bf16[4096,128]{1,0:T(8,128)(2,1)S(1)}, bf16[4096,128]{1,0:T(8,128)(2,1)S(1)}, bf16[4096,128]{1,0:T(8,128)(...) custom-call(bf16[256,2048]{1,0:T(8,128)(2,1)S(1)} %bitcast.11, bf16[256,2048]{1,0:T(8,128)(2,1)S(1)} %bitcast.12, ...), custom_call_target="tpu_custom_call" | custom-call | tf_op jit(solution)/shard_map/bring_in/pallas_call | solution.py:214
  73.6 0.0 copy-start.5
  73.6 1.0 copy-done.5
  74.6 37.7 %attention.1 = (bf16[4096,128]{1,0:T(8,128)(2,1)S(1)}, bf16[4096,128]{1,0:T(8,128)(2,1)S(1)}, bf16[4096,128]{1,0:T(8,128)(2,1)S(1)}, bf16[4096,128]{1,0:T(8,128)(2,1)S(1)}) custom-call(s32[512]{0:T(512)S(1)} %reshape.22.pat_ref, s32[32]{0:T(128)S(1)} %dynamic-slice_bitcast_fusion.live_ref, bf16[4096,128]{1,0:T(8,128)(2,1)S(1)} %get-tuple-element.20.q_ref, ...), custom_call_target="tpu_custom_call" | custom-call | tf_op jit(solution)/shard_map/attention/pallas_call | solution.py:449
  112.3 0.0 copy-start.6
  112.3 1.0 copy-done.6
  113.3 0.0 copy-start.7
  113.3 1.0 copy-done.7
  114.2 0.0 copy-start.8
  114.2 1.0 copy-done.8
  115.2 84.2 %take_home.1 = (bf16[256,2048]{1,0:T(8,128)(2,1)S(1)}, bf16[256,2048]{1,0:T(8,128)(2,1)S(1)}, bf16[256,2048]{1,0:T(8,128)(2,1)S(1)}, bf16[256,2048]{1,0:T(8,128)(2,1)S(1)}, f32[128,256]{1,0:T(8,128)S(1)}) custom-call(bf16[4096,128]{1,0:T(8,128)(2,1)S(1)} %get-tuple-element.24.o_ref, bf16[4096,128]{1,0:T(8,128)(2,1)} %copy-done.6, ...), custom_call_target="tpu_custom_call" | custom-call | tf_op jit(solution)/shard_map/take_home/pallas_call | solution.py:353
  199.4 1.0 copy.19
  200.4 1.0 copy.20
  201.3 1.0 copy.21
  202.3 1.0 copy.22
  203.3 0.7 copy.23
  (1 shorter events, 0.0 us)
Async XLA Ops:
  0.6 1.4 copy-start
  3.6 1.2 copy-start.1
  4.8 1.2 copy-start.2
  6.1 1.2 copy-start.3
  7.3 1.2 copy-start.4
  73.6 1.0 copy-start.5
  112.3 1.0 copy-start.6
  113.3 1.0 copy-start.7
  114.2 1.0 copy-start.8

commit v2 on v1

--- a/solution.py
+++ b/solution.py
@@ -219,29 +219,44 @@
         scratch_shapes=[
             pltpu.VMEM((ndp, rows, width), BF), pltpu.VMEM((mine, width), BF), pltpu.VMEM((mine, width), BF),
             dma((4, nseq)), dma((4, nseq)), dma((6,)), dma((6,)), dma((8,)), dma((8,)), dma((ndp,)), dma((ndp,)), dma((7,)), dma((ndp,))],
-        compiler_params=pltpu.CompilerParams(collective_id=0, has_side_effects=True, vmem_limit_bytes=40 * 2**20),
+        compiler_params=pltpu.CompilerParams(collective_id=0, has_side_effects=True, vmem_limit_bytes=60 * 2**20),
         name="bring_in",
     )(q, k, v, w, m)
 
 
 def take(factor, o_ref, dq_ref, dk_ref, dv_ref, wf_ref, mc_ref, out_ref, oq_ref, ok_ref, ov_ref, wg_ref,
-         a_buf, w_buf, c_buf, ct_buf, sum_buf, p_buf, part_buf, out_buf, wg_buf,
+         a_buf, w_buf, c_buf, ct_buf, p_buf, part_buf, out_buf, wg_buf,
          o_send, o_recv, g_send, g_recv, r_send, r_recv, f_send, f_recv, p_send, p_recv, local):
     dp, seq = lax.axis_index("dp"), lax.axis_index("seq")
     ndp, nseq = lax.axis_size("dp"), lax.axis_size("seq")
+    chips = ndp // 2
+    z, core = dp // 2, lax.rem(dp, 2)
     mine, width = a_buf.shape[1:]
     rows = width // ndp
     tensors = ((dq_ref, oq_ref), (dk_ref, ok_ref), (dv_ref, ov_ref))
     greet(dp, seq, ndp, nseq)
 
-    def column_half(ref, half):
-        return ref.at[:, pl.ds(half * (width // 2), width // 2)]
-
-    ring = Ring(column_half, a_buf, dp, seq, ndp, r_send, r_recv, f_send, f_recv)
+    def slot(offset, other=False):
+        return lax.rem(z + chips + offset, chips) * 2 + (1 - core if other else core)
+
+    def head_at(step):
+        return lax.rem(seq + nseq - step, nseq)
 
     def home(other, source):
         return pltpu.make_async_remote_copy(o_ref.at[columns(other, mine), :], a_buf.at[dp].at[:, columns(source, HD)],
                                             o_send.at[other], o_recv.at[source], device_id=(dp, other), device_id_type=MESH)
+
+    def hop(kind, step):
+        way = (1, -1, 1 - 2 * lax.rem(step, 2))[kind]
+        origin = slot(0) if kind < 2 else slot(-way)
+        piece = a_buf.at[origin].at[:, columns(head_at(step), HD)]
+        return pltpu.make_async_remote_copy(piece, piece, r_send.at[kind, step], r_recv.at[kind, step],
+                                            device_id=(slot(way), seq), device_id_type=MESH)
+
+    def hand(kind, step):
+        piece = a_buf.at[slot((0, -1, 1, 2)[kind])].at[:, columns(head_at(step), HD)]
+        return pltpu.make_async_remote_copy(piece, piece, f_send.at[kind, step], f_recv.at[kind, step],
+                                            device_id=(slot(0, True), seq), device_id_type=MESH)
 
     def spread(which, step):
         src, dst = tensors[which]
@@ -253,15 +268,21 @@
         src, dst = tensors[which]
         return pltpu.make_async_copy(src.at[columns(seq, mine), :], dst.at[:, columns(seq, HD)], local.at[which])
 
+    def share(head, source):
+        return pltpu.make_async_remote_copy(p_buf.at[:, columns(head, HD)], part_buf.at[source],
+                                            p_send.at[head], p_recv.at[source], device_id=(dp, head), device_id_type=MESH)
+
+    own_p = pltpu.make_async_copy(p_buf.at[:, columns(seq, HD)], part_buf.at[seq], local.at[7])
     own_o = pltpu.make_async_copy(o_ref.at[columns(seq, mine), :], a_buf.at[dp].at[:, columns(seq, HD)], local.at[3])
     own_c = pltpu.make_async_copy(mc_ref, c_buf, local.at[4])
     own_w = pltpu.make_async_copy(wf_ref, w_buf, local.at[5])
+    own_out = pltpu.make_async_copy(out_buf, out_ref, local.at[6])
+    own_o.start()
 
     @pl.loop(1, nseq)
     def _(step):
         home(lax.rem(seq + step, nseq), seq).start()
 
-    own_o.start()
     own_c.start()
     own_w.start()
     for which in range(3):
@@ -271,17 +292,52 @@
         keep(which).start()
 
     own_c.wait()
-    for slot in range(ndp):
-        ct_buf[slot] = c_buf[slot].T
-    sum_buf[...] = jnp.zeros_like(sum_buf)
+    for source in range(ndp):
+        ct_buf[:, source * mine:(source + 1) * mine] = c_buf[source].T
     own_o.wait()
-    for half in range(2):
-        @pl.loop(half * (nseq // 2), (half + 1) * (nseq // 2))
-        def _(other):
-            @pl.when(other != seq)
+
+    @pl.loop(0, nseq + 3)
+    def _(turn):
+        @pl.when(turn < nseq)
+        def _():
+            @pl.when(turn > 0)
             def _():
-                home(other, other).wait_recv()
-        ring.start(half)
+                home(head_at(turn), head_at(turn)).wait_recv()
+            hop(0, turn).start()
+            hop(1, turn).start()
+            hand(0, turn).start()
+
+        @pl.when((turn >= 1) & (turn < nseq + 1))
+        def _():
+            step = turn - 1
+            hop(0, step).wait_recv()
+            hop(1, step).wait_recv()
+            hop(2, step).start()
+            hand(1, step).start()
+            hand(2, step).start()
+
+        @pl.when((turn >= 2) & (turn < nseq + 2))
+        def _():
+            step = turn - 2
+            hop(2, step).wait_recv()
+            hand(3, step).start()
+
+        @pl.when(turn >= 3)
+        def _():
+            step = turn - 3
+            for kind in range(4):
+                hand(kind, step).wait_recv()
+            at = columns(head_at(step), HD)
+            pieces = a_buf[:, :, at].reshape(ndp * mine, HD)
+            p_buf[:, at] = jnp.dot(ct_buf[...], pieces, preferred_element_type=jnp.float32).astype(BF)
+
+            @pl.when(step > 0)
+            def _():
+                share(head_at(step), seq).start()
+
+            @pl.when(step == 0)
+            def _():
+                own_p.start()
 
     own_w.wait()
 
@@ -289,57 +345,38 @@
     def _(tile):
         at = columns(tile, rows)
         total = jnp.zeros((mine, rows), jnp.float32)
-        for slot in range(ndp):
-            total += jnp.dot(a_buf[dp, :, slot * rows:(slot + 1) * rows], w_buf[slot, :, at], preferred_element_type=jnp.float32)
+        for source in range(ndp):
+            total += jnp.dot(a_buf[dp, :, source * rows:(source + 1) * rows], w_buf[source, :, at], preferred_element_type=jnp.float32)
         out_buf[:, at] = total.astype(BF)
 
-    own_out = pltpu.make_async_copy(out_buf, out_ref, local.at[6])
     own_out.start()
-
-    def use(slot):
-        @pl.loop(0, ndp)
-        def _(tile):
-            at = columns(tile, rows)
-            sum_buf[:, at] += jnp.dot(ct_buf[slot], a_buf[slot, :, at], preferred_element_type=jnp.float32)
-
-    ring.run(use)
-    p_buf[...] = sum_buf[...].astype(BF)
-
-    def share(head, source):
-        return pltpu.make_async_remote_copy(p_buf.at[:, columns(head, HD)], part_buf.at[source],
-                                            p_send.at[head], p_recv.at[source], device_id=(dp, head), device_id_type=MESH)
-
-    own_p = pltpu.make_async_copy(p_buf.at[:, columns(seq, HD)], part_buf.at[seq], local.at[7])
+    own_p.wait()
+    wg_buf[...] = part_buf[seq].astype(jnp.float32)
 
     @pl.loop(1, nseq)
     def _(step):
-        share(lax.rem(seq + step, nseq), seq).start()
-
-    own_p.start()
-    own_out.wait()
+        source = lax.rem(seq + step, nseq)
+        share(source, source).wait_recv()
+        wg_buf[...] += part_buf[source].astype(jnp.float32)
+
+    wg_ref[...] = wg_buf[...].T * factor
     for which in range(3):
         @pl.loop(1, nseq)
         def _(step):
             spread(which, step).wait()
         keep(which).wait()
 
-    own_p.wait()
-
     @pl.loop(0, nseq)
-    def _(other):
-        @pl.when(other != seq)
+    def _(step):
+        @pl.when(step > 0)
         def _():
-            home(other, seq).wait_send()
-            share(other, seq).wait_send()
-            share(other, other).wait_recv()
-
-    total = part_buf[0].astype(jnp.float32)
-    for source in range(1, nseq):
-        total += part_buf[source].astype(jnp.float32)
-    wg_buf[...] = total.T * factor
-    last = pltpu.make_async_copy(wg_buf, wg_ref, local.at[8])
-    last.start()
-    last.wait()
+            home(head_at(step), seq).wait_send()
+            share(head_at(step), seq).wait_send()
+        for kind in range(3):
+            hop(kind, step).wait_send()
+        for kind in range(4):
+            hand(kind, step).wait_send()
+    own_out.wait()
 
 
 def take_home(o, dq, dk, dv, wf, mc):
@@ -354,14 +391,14 @@
         functools.partial(take, factor),
         out_shape=(out,) * 4 + (jax.ShapeDtypeStruct((HD, rows), jnp.float32),),
         in_specs=[place] * 6,
-        out_specs=(place,) * 5,
+        out_specs=(place,) * 4 + (pl.BlockSpec(memory_space=pltpu.VMEM),),
         scratch_shapes=[
             pltpu.VMEM((ndp, mine, width), BF), pltpu.VMEM((ndp, rows, width), BF), pltpu.VMEM((ndp, mine, rows), BF),
-            pltpu.VMEM((ndp, rows, mine), BF), pltpu.VMEM((rows, width), jnp.float32), pltpu.VMEM((rows, width), BF),
-            pltpu.VMEM((nseq, rows, HD), BF), pltpu.VMEM((mine, width), BF), pltpu.VMEM((HD, rows), jnp.float32),
-            dma((nseq,)), dma((nseq,)), dma((3, nseq)), dma((3, nseq)), dma((6,)), dma((6,)), dma((8,)), dma((8,)),
-            dma((nseq,)), dma((nseq,)), dma((9,))],
-        compiler_params=pltpu.CompilerParams(collective_id=1, has_side_effects=True, vmem_limit_bytes=48 * 2**20),
+            pltpu.VMEM((rows, ndp * mine), BF), pltpu.VMEM((rows, width), BF),
+            pltpu.VMEM((nseq, rows, HD), BF), pltpu.VMEM((mine, width), BF), pltpu.VMEM((rows, HD), jnp.float32),
+            dma((nseq,)), dma((nseq,)), dma((3, nseq)), dma((3, nseq)), dma((3, nseq)), dma((3, nseq)), dma((4, nseq)), dma((4, nseq)),
+            dma((nseq,)), dma((nseq,)), dma((8,))],
+        compiler_params=pltpu.CompilerParams(collective_id=1, has_side_effects=True, vmem_limit_bytes=60 * 2**20),
         name="take_home",
     )(o, dq, dk, dv, wf, mc)
 
@@ -455,7 +492,7 @@
             pltpu.VMEM((length, HD), BF), pltpu.VMEM((length, HD), BF),
             pltpu.VMEM((length, 2 * HD), jnp.float32),
             pltpu.VMEM((KMAX * BLOCK, BLOCK), jnp.float32), pltpu.VMEM((KMAX * BLOCK, BLOCK), jnp.float32)],
-        compiler_params=pltpu.CompilerParams(vmem_limit_bytes=40 * 2**20),
+        compiler_params=pltpu.CompilerParams(vmem_limit_bytes=60 * 2**20),
         name="attention",
     )(pat.reshape(-1), live, q, k, v, d)
 

time: 207 us -> 207 us (level); the launches traced: 204 us -> 206 us
  Pallas kernels: 187 us -> 191 us
  local copies, waits for them, and re-layouts: 14.2 us -> 11.9 us
    pallas_call x1, Pallas kernels: 84.2 us -> 94.4 us  [take_home(): pl.pallas_call(functools.partial(take, factor), out_shape=(out,) * 4 + (j...]
    pallas_call x1, Pallas kernels: 37.7 us -> 30.9 us  [attention(): pl.pallas_call(functools.partial(attend, STEP), out_shape=(out,) * 4, in_...]
    unnamed x23 -> x9, local copies, waits for them, and re-layouts: 13.3 us -> 9.92 us
where the time goes in v2:
time: 207 us; the launch traced here: 206 us
  Pallas kernels  191 us (92%)
  local copies, waits for them, and re-layouts  11.9 us (6%)
  other arithmetic  3.06 us (1%)
    pallas_call x1, Pallas kernels, take_home(): pl.pallas_call(functools.partial(take, factor), out_shape=(out,) * 4 + (j...  94.4 us
    pallas_call x1, Pallas kernels, bring_in(): pl.pallas_call(bring, out_shape=(head,) * 4 + (jax.ShapeDtypeStruct((ndp,...  65.3 us
    pallas_call x1, Pallas kernels, attention(): pl.pallas_call(functools.partial(attend, STEP), out_shape=(out,) * 4, in_...  30.9 us
    unnamed x9, local copies, waits for them, and re-layouts  9.92 us

profile of v2, /device:TPU:1, one launch (start us, length us, event | category | flops | bytes accessed | tf_op | source)
XLA Modules:
  0.0 206.2 jit_solution(1568520366479101472)
XLA Ops:
  0.6 0.0 copy-start
  0.7 0.7 convert_reduce_fusion
  1.4 1.2 dynamic-slice_bitcast_fusion.live_ref
  2.6 0.0 copy-done
  2.6 0.1 copy.13
  2.7 0.7 reshape.22.pat_ref
  3.4 2.3 %bitcast_multiply_fusion.m_ref = bf16[256,2048]{1,0:T(8,128)(2,1)} fusion(bf16[1,256,2048]{2,1,0:T(8,128)(2,1)} %param.12, bf16[256]{0:T(256)(128)(2,1)S(1)} %convert_reduce_fusion), kind=kLoop, calls=%fused_computation | loop fusion | flops 524288 | bytes 2097664 | tf_op jit(solution)/shard_map/mul | solution.py:504
  5.7 65.3 %bring_in.1 = (bf16[4096,128]{1,0:T(8,128)(2,1)}, bf16[4096,128]{1,0:T(8,128)(2,1)}, bf16[4096,128]{1,0:T(8,128)(2,1)}, bf16[4096,128]{1,0:T(8,128)(2,1)}, bf16[...) custom-call(bf16[256,2048]{1,0:T(8,128)(2,1)} %bitcast.11, bf16[256,2048]{1,0:T(8,128)(2,1)} %bitcast.12, ...), custom_call_target="tpu_custom_call" | custom-call | tf_op jit(solution)/shard_map/bring_in/pallas_call | solution.py:214
  71.0 30.9 %attention.1 = (bf16[4096,128]{1,0:T(8,128)(2,1)}, bf16[4096,128]{1,0:T(8,128)(2,1)}, bf16[4096,128]{1,0:T(8,128)(2,1)}, bf16[4096,128]{1,0:T(8,128)(2,1)}) custom-call(s32[512]{0:T(512)} %reshape.22.pat_ref, s32[32]{0:T(128)} %dynamic-slice_bitcast_fusion.live_ref, bf16[4096,128]{1,0:T(8,128)(2,1)} %get-tuple-element.20.q_ref, ...), custom_call_target="tpu_custom_call" | custom-call | tf_op jit(solution)/shard_map/attention/pallas_call | solution.py:486
  101.9 94.4 %take_home.1 = (bf16[256,2048]{1,0:T(8,128)(2,1)}, bf16[256,2048]{1,0:T(8,128)(2,1)}, bf16[256,2048]{1,0:T(8,128)(2,1)}, bf16[256,2048]{1,0:T(8,128)(2,1)}, f32[128,256]{1,0:T(8,128)}) custom-call(bf16[4096,128]{1,0:T(8,128)(2,1)} %get-tuple-element.24.o_ref, bf16[4096,128]{1,0:T(8,128)(2,1)} %get-tuple-element.25.dq_ref, ...), custom_call_target="tpu_custom_call" | custom-call | tf_op jit(solution)/shard_map/take_home/pallas_call | solution.py:390
  196.3 0.0 copy-start.1
  196.3 2.3 %copy.19 = bf16[1,256,2048]{2,1,0:T(8,128)(2,1)} copy(bf16[1,256,2048]{2,1,0:T(8,128)(2,1)} %bitcast.17) | data formatting | bytes 2097152
  198.6 2.3 %copy.20 = bf16[1,256,2048]{2,1,0:T(8,128)(2,1)} copy(bf16[1,256,2048]{2,1,0:T(8,128)(2,1)} %bitcast.16) | data formatting | bytes 2097152
  200.9 2.3 %copy.21 = bf16[1,256,2048]{2,1,0:T(8,128)(2,1)} copy(bf16[1,256,2048]{2,1,0:T(8,128)(2,1)} %bitcast.15) | data formatting | bytes 2097152
  203.3 2.3 %copy.22 = bf16[1,256,2048]{2,1,0:T(8,128)(2,1)} copy(bf16[1,256,2048]{2,1,0:T(8,128)(2,1)} %bitcast.14) | data formatting | bytes 2097152
  205.6 0.0 copy-done.1
  205.6 0.7 copy.23
  (1 shorter events, 0.0 us)
Async XLA Ops:
  0.6 2.0 copy-start
  196.3 9.3 %copy-start.1 = (f32[128,256]{1,0:T(8,128)S(1)}, f32[128,256]{1,0:T(8,128)}, u32[]{:S(2)}) copy-start(f32[128,256]{1,0:T(8,128)} %get-tuple-element.44) | copy-start | bytes 393220

commit v3 on v2

--- a/solution.py
+++ b/solution.py
@@ -11,7 +11,10 @@
 HD = 128
 BLOCK = 128
 KMAX = 16
-STEP = 4
+STEP = 2
+GROUP = 2
+PAIR = 4
+UNROLL = 4
 SCALE = 1.0 / math.sqrt(HD)
 BF = jnp.bfloat16
 MESH = pl.DeviceIdType.MESH
@@ -74,7 +77,7 @@
             self.hop(index, source).start()
         self.hand(half, source).start()
 
-    def run(self, use):
+    def run(self, use, late):
         use(self.slot(0))
         for index in (0, 1):
             self.hop(index).wait_recv()
@@ -94,6 +97,7 @@
         for index in (4, 5):
             self.hop(index).wait_recv()
             self.hand(index + 2).start()
+        late()
         use(self.slot(2))
         self.hand(6).wait_recv()
         self.hand(7).wait_recv()
@@ -104,7 +108,7 @@
             self.hand(index).wait_send()
 
 
-def bring(q_ref, k_ref, v_ref, w_ref, m_ref, hq_ref, hk_ref, hv_ref, hd_ref, wf_ref, mc_ref,
+def bring(mask_ref, q_ref, k_ref, v_ref, w_ref, m_ref, hq_ref, hk_ref, hv_ref, hd_ref, wf_ref, mc_ref,
           w_buf, m_buf, g_buf, a_send, a_recv, w_send, w_recv, f_send, f_recv, m_send, m_recv, local, keep_w):
     dp, seq = lax.axis_index("dp"), lax.axis_index("seq")
     ndp, nseq = lax.axis_size("dp"), lax.axis_size("seq")
@@ -119,7 +123,7 @@
 
     def sides(step):
         other = lax.rem(dp + step, ndp)
-        return pltpu.make_async_remote_copy(m_ref.at[:, columns(other, rows)], mc_ref.at[dp], m_send.at[step], m_recv.at[step],
+        return pltpu.make_async_remote_copy(m_buf.at[:, columns(other, rows)], mc_ref.at[dp], m_send.at[step], m_recv.at[step],
                                             device_id=(other, seq), device_id_type=MESH)
 
     def spread(which, step):
@@ -134,7 +138,7 @@
 
     own_w = pltpu.make_async_copy(w_ref, w_buf.at[dp], local.at[3])
     own_m = pltpu.make_async_copy(m_ref, m_buf, local.at[4])
-    own_c = pltpu.make_async_copy(m_ref.at[:, columns(dp, rows)], mc_ref.at[dp], local.at[5])
+    own_c = pltpu.make_async_copy(m_buf.at[:, columns(dp, rows)], mc_ref.at[dp], local.at[5])
     own_w.start()
     own_m.start()
     ring.start(0, w_ref)
@@ -144,13 +148,17 @@
         def _(step):
             spread(which, step).start()
         keep(which).start()
+    own_m.wait()
+    for first in range(0, mine, HD):
+        seen = jnp.broadcast_to(mask_ref[:, first:first + HD].astype(jnp.float32), (HD, HD)).T.astype(BF)
+        for left in range(0, m_buf.shape[1], HD):
+            m_buf[first:first + HD, left:left + HD] *= seen
     own_c.start()
 
-    @pl.loop(1, ndp)
-    def _(step):
-        sides(step).start()
-
-    own_m.wait()
+    def late():
+        @pl.loop(1, ndp)
+        def _(step):
+            sides(step).start()
 
     def store(slot):
         return pltpu.make_async_copy(w_buf.at[slot], wf_ref.at[slot], keep_w.at[slot])
@@ -177,7 +185,7 @@
                 own_g().start()
 
     own_w.wait()
-    ring.run(use)
+    ring.run(use, late)
     own_c.wait()
 
     @pl.loop(1, ndp)
@@ -204,7 +212,7 @@
             give(other, other).wait_recv()
 
 
-def bring_in(q, k, v, w, m):
+def bring_in(mask, q, k, v, w, m):
     ndp, nseq = lax.axis_size("dp"), lax.axis_size("seq")
     mine, width = q.shape
     rows = w.shape[0]
@@ -214,14 +222,14 @@
     return pl.pallas_call(
         bring,
         out_shape=(head,) * 4 + (jax.ShapeDtypeStruct((ndp, rows, width), BF), jax.ShapeDtypeStruct((ndp, mine, rows), BF)),
-        in_specs=[place] * 5,
+        in_specs=[pl.BlockSpec(memory_space=pltpu.VMEM)] + [place] * 5,
         out_specs=(place,) * 6,
         scratch_shapes=[
             pltpu.VMEM((ndp, rows, width), BF), pltpu.VMEM((mine, width), BF), pltpu.VMEM((mine, width), BF),
             dma((4, nseq)), dma((4, nseq)), dma((6,)), dma((6,)), dma((8,)), dma((8,)), dma((ndp,)), dma((ndp,)), dma((7,)), dma((ndp,))],
         compiler_params=pltpu.CompilerParams(collective_id=0, has_side_effects=True, vmem_limit_bytes=60 * 2**20),
         name="bring_in",
-    )(q, k, v, w, m)
+    )(mask, q, k, v, w, m)
 
 
 def take(factor, o_ref, dq_ref, dk_ref, dv_ref, wf_ref, mc_ref, out_ref, oq_ref, ok_ref, ov_ref, wg_ref,
@@ -402,80 +410,126 @@
         name="take_home",
     )(o, dq, dk, dv, wf, mc)
 
-def attend(step, pat_ref, live_ref, q_ref, k_ref, v_ref, d_ref, o_ref, dq_ref, dk_ref, dv_ref, kt_ref, vt_ref, acc_ref, e_ref, g_ref):
+def attend(pat_ref, live_ref, q_ref, k_ref, v_ref, d_ref, o_ref, dq_ref, dk_ref, dv_ref, kt_ref, vt_ref, acc_ref, e_ref, g_ref, order_ref, fill_ref):
     nb = q_ref.shape[0] // BLOCK
-    fold = lambda x: x.reshape(BLOCK // 8, 8, BLOCK)
-
+    me = lax.axis_index("seq")
+    levels = KMAX // STEP
+
+    def block(index):
+        return pl.ds(pl.multiple_of(index * BLOCK, BLOCK), BLOCK)
+
+    def fold(x):
+        return x.reshape(-1, 8, x.shape[-1])
+
+    for level in range(levels):
+        fill_ref[level] = 0
     @pl.loop(0, nb)
     def _(b):
-        rows = pl.ds(pl.multiple_of(b * BLOCK, BLOCK), BLOCK)
-        kt_ref[rows, :] = k_ref[rows, :].T
-        vt_ref[rows, :] = v_ref[rows, :].T
-        acc_ref[rows, :] = jnp.zeros((BLOCK, 2 * HD), jnp.float32)
-
-    def with_slots(count, b):
-        rows = pl.ds(pl.multiple_of(b * BLOCK, BLOCK), BLOCK)
-        live = live_ref[b]
-        q = q_ref[rows, :]
-        d = d_ref[rows, :]
-        none = jnp.zeros((BLOCK, HD), BF)
+        level = (live_ref[me, b] - 1) // STEP
+        for later in range(1, levels):
+            @pl.when(level < later)
+            def _():
+                fill_ref[later] += 1
+    @pl.loop(0, nb)
+    def _(b):
+        level = (live_ref[me, b] - 1) // STEP
+        order_ref[fill_ref[level]] = b
+        fill_ref[level] += 1
+
+    @pl.loop(0, nb // UNROLL)
+    def _(turn):
+        for i in range(UNROLL):
+            rows = block(turn * UNROLL + i)
+            kt_ref[rows, :] = k_ref[rows, :].T
+            vt_ref[rows, :] = v_ref[rows, :].T
+            acc_ref[rows, :] = jnp.zeros((BLOCK, 2 * HD), jnp.float32)
+
+    none = jnp.zeros((BLOCK, HD), BF)
+
+    def scores(count, b, at, base):
+        live = live_ref[me, b]
+        q = q_ref[block(b), :]
+        d = d_ref[block(b), :]
         enter = jnp.concatenate([jnp.concatenate([q, none], 1), jnp.concatenate([none, d], 1)], 0)
-        leave = jnp.concatenate([jnp.concatenate([d, none], 1), jnp.concatenate([none, q], 1)], 0)
-        at = [pl.ds(pl.multiple_of(pat_ref[b * KMAX + j] * BLOCK, BLOCK), BLOCK) for j in range(count)]
         top = jnp.full((8, BLOCK), -1e30, jnp.float32)
         total = jnp.zeros((8, BLOCK), jnp.float32)
         mixed = jnp.zeros((8, BLOCK), jnp.float32)
         tops = []
-        for j in range(count):
-            both = lax.dot_general(jnp.concatenate([k_ref[at[j], :], v_ref[at[j], :]], 1), enter,
-                                   (((1,), (1,)), ((), ())), preferred_element_type=jnp.float32)
+        for j in range(0, count, GROUP):
+            many = min(GROUP, count - j)
+            both = lax.dot_general(
+                jnp.concatenate([jnp.concatenate([k_ref[at[i], :], v_ref[at[i], :]], 1) for i in range(j, j + many)], 0),
+                enter, NT, preferred_element_type=jnp.float32)
             s, g = both[:, :BLOCK], both[:, BLOCK:]
-            if j > count - step:
-                s = jnp.where(j < live, s, jnp.float32(-1e30))
+            if j + many > 1:
+                parts = []
+                for i in range(many):
+                    part = s[i * BLOCK:(i + 1) * BLOCK]
+                    parts.append(jnp.where(j + i < live, part, jnp.float32(-1e30)) if j + i > 0 else part)
+                s = jnp.concatenate(parts, 0)
             new = jnp.maximum(top, jnp.max(fold(s), axis=0))
             old = jnp.exp((top - new) * SCALE)
             e = jnp.exp((fold(s) - new[None]) * SCALE)
             total = total * old + jnp.sum(e, axis=0)
             mixed = mixed * old + jnp.sum(e * fold(g), axis=0)
-            e_ref[j * BLOCK:(j + 1) * BLOCK, :] = e.reshape(BLOCK, BLOCK)
-            g_ref[j * BLOCK:(j + 1) * BLOCK, :] = g
-            tops.append(new)
+            e_ref[base + j * BLOCK:base + (j + many) * BLOCK, :] = e.reshape(many * BLOCK, BLOCK)
+            g_ref[base + j * BLOCK:base + (j + many) * BLOCK, :] = g
+            tops += [new] * many
             top = new
         peak = jnp.max(top, axis=0, keepdims=True)
         level = jnp.exp((top - peak) * SCALE)
         inverse = 1.0 / jnp.sum(total * level, axis=0, keepdims=True)
         delta = jnp.sum(mixed * level, axis=0, keepdims=True) * inverse
+        return tops, peak, inverse, delta
+
+    def grads(count, b, at, base, tops, peak, inverse, delta):
+        q = q_ref[block(b), :]
+        d = d_ref[block(b), :]
+        leave = jnp.concatenate([jnp.concatenate([d, none], 1), jnp.concatenate([none, q], 1)], 0)
         o_sum = jnp.zeros((HD, BLOCK), jnp.float32)
         q_sum = jnp.zeros((HD, BLOCK), jnp.float32)
-        for j in range(0, count, 2):
+        for j in range(0, count, GROUP):
+            many = min(GROUP, count - j)
             probs, slopes = [], []
-            for i in (j, j + 1):
-                e = e_ref[i * BLOCK:(i + 1) * BLOCK, :]
-                g = g_ref[i * BLOCK:(i + 1) * BLOCK, :]
+            for i in range(j, j + many):
+                e = e_ref[base + i * BLOCK:base + (i + 1) * BLOCK, :]
+                g = g_ref[base + i * BLOCK:base + (i + 1) * BLOCK, :]
                 weight = jnp.exp((tops[i] - peak) * SCALE) * inverse
                 p = (fold(e) * weight[None]).reshape(BLOCK, BLOCK)
-                pb = p.astype(BF)
-                sb = (p * (g - delta)).astype(BF)
-                acc_ref[at[i], :] += jnp.dot(jnp.concatenate([pb, sb], 1), leave, preferred_element_type=jnp.float32)
-                probs.append(pb)
-                slopes.append(sb)
-            o_sum += jnp.dot(jnp.concatenate([vt_ref[at[j], :], vt_ref[at[j + 1], :]], 1),
-                             jnp.concatenate(probs, 0), preferred_element_type=jnp.float32)
-            q_sum += jnp.dot(jnp.concatenate([kt_ref[at[j], :], kt_ref[at[j + 1], :]], 1),
-                             jnp.concatenate(slopes, 0), preferred_element_type=jnp.float32)
-        o_ref[rows, :] = o_sum.T.astype(BF)
-        dq_ref[rows, :] = (q_sum.T * SCALE).astype(BF)
-
-    @pl.loop(0, nb)
-    def _(b):
-        branches = [functools.partial(with_slots, c) for c in range(step, KMAX + 1, step)]
-        lax.switch((live_ref[b] - 1) // step, branches, b)
-
-    @pl.loop(0, nb)
-    def _(b):
-        rows = pl.ds(pl.multiple_of(b * BLOCK, BLOCK), BLOCK)
-        dv_ref[rows, :] = acc_ref[rows, :HD].astype(BF)
-        dk_ref[rows, :] = (acc_ref[rows, HD:] * SCALE).astype(BF)
+                probs.append(p.astype(BF))
+                slopes.append((p * (g - delta)).astype(BF))
+            pb, sb = jnp.concatenate(probs, 0), jnp.concatenate(slopes, 0)
+            ps = jnp.concatenate([pb, sb], 1)
+            out = jnp.dot(ps, leave, preferred_element_type=jnp.float32)
+            for i in range(many):
+                acc_ref[at[j + i], :] += out[i * BLOCK:(i + 1) * BLOCK]
+            vt = jnp.concatenate([vt_ref[at[i], :] for i in range(j, j + many)], 1)
+            kt = jnp.concatenate([kt_ref[at[i], :] for i in range(j, j + many)], 1)
+            two = jnp.dot(jnp.concatenate([vt, kt], 0), ps, preferred_element_type=jnp.float32)
+            o_sum += two[:HD, :BLOCK]
+            q_sum += two[HD:, BLOCK:]
+        o_ref[block(b), :] = o_sum.T.astype(BF)
+        dq_ref[block(b), :] = (q_sum.T * SCALE).astype(BF)
+
+    def with_slots(count, turn):
+        bs = [order_ref[turn * PAIR + i] for i in range(PAIR)]
+        ats = [[block(pat_ref[b, j]) for j in range(count)] for b in bs]
+        states = [scores(count, b, at, i * KMAX * BLOCK) for i, (b, at) in enumerate(zip(bs, ats))]
+        for i, (b, at, state) in enumerate(zip(bs, ats, states)):
+            grads(count, b, at, i * KMAX * BLOCK, *state)
+
+    @pl.loop(0, nb // PAIR)
+    def _(turn):
+        branches = [functools.partial(with_slots, c) for c in range(STEP, KMAX + 1, STEP)]
+        longest = live_ref[me, order_ref[turn * PAIR + PAIR - 1]]
+        lax.switch((longest - 1) // STEP, branches, turn)
+
+    @pl.loop(0, nb // UNROLL)
+    def _(turn):
+        for i in range(UNROLL):
+            rows = block(turn * UNROLL + i)
+            dv_ref[rows, :] = acc_ref[rows, :HD].astype(BF)
+            dk_ref[rows, :] = (acc_ref[rows, HD:] * SCALE).astype(BF)
 
 
 def attention(q, k, v, d, pat, live):
@@ -484,27 +538,49 @@
     vm = pl.BlockSpec(memory_space=pltpu.VMEM)
     sm = pl.BlockSpec(memory_space=pltpu.SMEM)
     return pl.pallas_call(
-        functools.partial(attend, STEP),
+        attend,
         out_shape=(out,) * 4,
         in_specs=[sm, sm, vm, vm, vm, vm],
         out_specs=(vm,) * 4,
         scratch_shapes=[
             pltpu.VMEM((length, HD), BF), pltpu.VMEM((length, HD), BF),
             pltpu.VMEM((length, 2 * HD), jnp.float32),
-            pltpu.VMEM((KMAX * BLOCK, BLOCK), jnp.float32), pltpu.VMEM((KMAX * BLOCK, BLOCK), jnp.float32)],
+            pltpu.VMEM((PAIR * KMAX * BLOCK, BLOCK), jnp.float32), pltpu.VMEM((PAIR * KMAX * BLOCK, BLOCK), jnp.float32),
+            pltpu.SMEM((length // BLOCK,), jnp.int32), pltpu.SMEM((KMAX // STEP,), jnp.int32)],
         compiler_params=pltpu.CompilerParams(vmem_limit_bytes=60 * 2**20),
         name="attention",
-    )(pat.reshape(-1), live, q, k, v, d)
+    )(pat, live, q, k, v, d)
+
+
+def pass_on(*refs):
+    arrays, sems = refs[:-1], refs[-1]
+    count = len(arrays) // 2
+    copies = [pltpu.make_async_copy(arrays[i], arrays[count + i], sems.at[i]) for i in range(count)]
+    for copy in copies:
+        copy.start()
+    for copy in copies:
+        copy.wait()
+
+
+def hand_over(*arrays):
+    place = pl.BlockSpec(memory_space=pl.ANY)
+    return pl.pallas_call(
+        pass_on,
+        out_shape=tuple(jax.ShapeDtypeStruct(x.shape, x.dtype) for x in arrays),
+        in_specs=[place] * len(arrays),
+        out_specs=(place,) * len(arrays),
+        scratch_shapes=[pltpu.SemaphoreType.DMA((len(arrays),))],
+        compiler_params=pltpu.CompilerParams(vmem_limit_bytes=60 * 2**20),
+        name="hand_over",
+    )(*arrays)
 
 
 def local(queries, keys, values, weight_out, cotangent, hidden_mask, pattern, live_slots):
     seq = lax.axis_index("seq")
     pat = lax.dynamic_index_in_dim(pattern, seq, 0, keepdims=False)
-    live = lax.dynamic_index_in_dim(live_slots, seq, 0, keepdims=False)
-    masked = cotangent[0] * hidden_mask[0][:, None].astype(BF)
-    q, k, v, d, weights, sides = bring_in(queries[0], keys[0], values[0], weight_out, masked)
-    attn, dq, dk, dv = attention(q, k, v, d, pat, live)
-    block_out, dq, dk, dv, weight_grad = take_home(attn, dq, dk, dv, weights, sides)
+    q, k, v, d, weights, sides = bring_in(hidden_mask, queries[0], keys[0], values[0], weight_out, cotangent[0])
+    attn, dq, dk, dv = attention(q, k, v, d, pat, live_slots)
+    block_out, dq, dk, dv, weight_grad = hand_over(*take_home(attn, dq, dk, dv, weights, sides))
     return (block_out[None], dq[None], dk[None], dv[None], weight_grad)
 
 

time: 207 us -> 313 us (1.51)
  Pallas kernels: 191 us -> 310 us
  local copies, waits for them, and re-layouts: 11.9 us -> 1.58 us
    pallas_call x1 -> x2, Pallas kernels: 30.9 us -> 160 us  [the longest x1 132 us: hand_over(): pl.pallas_call(pass_on, out_shape=tuple((jax.ShapeDtypeStruct(x.shape, x....]
    unnamed x9 -> x2, local copies, waits for them, and re-layouts: 9.92 us -> 0.9 us
    pallas_call x1, Pallas kernels: 94.4 us -> 89.1 us  [take_home(): pl.pallas_call(functools.partial(take, factor), out_shape=(out,) * 4 + (j...]
    pallas_call x1, Pallas kernels: 65.3 us -> 60.8 us  [bring_in(): pl.pallas_call(bring, out_shape=(head,) * 4 + (jax.ShapeDtypeStruct((ndp,...]
where the time goes in v3:
time: 313 us; the launch traced here: 312 us
  Pallas kernels  310 us (99%)
    pallas_call x1, Pallas kernels, hand_over(): pl.pallas_call(pass_on, out_shape=tuple((jax.ShapeDtypeStruct(x.shape, x....  132 us
    pallas_call x1, Pallas kernels, take_home(): pl.pallas_call(functools.partial(take, factor), out_shape=(out,) * 4 + (j...  89.1 us
    pallas_call x1, Pallas kernels, bring_in(): pl.pallas_call(bring, out_shape=(head,) * 4 + (jax.ShapeDtypeStruct((ndp,...  60.8 us
    pallas_call x1, Pallas kernels, attention(): pl.pallas_call(attend, out_shape=(out,) * 4, in_specs=[sm, sm, vm, vm, vm...  27.7 us

profile of v3, /device:TPU:1, one launch (start us, length us, event | category | flops | bytes accessed | tf_op | source)
XLA Modules:
  0.0 312.3 jit_solution(7038848843885019454)
XLA Ops:
  0.6 0.0 copy-start
  0.6 0.9 copy-done
  1.5 0.7 copy.13
  2.2 60.8 %bring_in.1 = (bf16[4096,128]{1,0:T(8,128)(2,1)}, bf16[4096,128]{1,0:T(8,128)(2,1)}, bf16[4096,128]{1,0:T(8,128)(2,1)}, bf16[4096,128]{1,0:T(8,128)(2,1)}, bf16[...) custom-call(s32[1,256]{1,0:T(1,128)} %mask_ref.1, bf16[256,2048]{1,0:T(8,128)(2,1)} %bitcast.9, ...), custom_call_target="tpu_custom_call" | custom-call | tf_op jit(solution)/shard_map/bring_in/pallas_call | solution.py:222
  63.1 27.7 %attention.1 = (bf16[4096,128]{1,0:T(8,128)(2,1)}, bf16[4096,128]{1,0:T(8,128)(2,1)}, bf16[4096,128]{1,0:T(8,128)(2,1)}, bf16[4096,128]{1,0:T(8,128)(2,1)}) custom-call(s32[32,16]{1,0:T(8,128)} %bitcast.13, s32[16,32]{1,0:T(8,128)} %live_ref.1, bf16[4096,128]{1,0:T(8,128)(2,1)} %get-tuple-element.25.q_ref, bf16[4096,128]{1,0:T(8,128)(2,1)} %get-tuple-element.26.k_ref, ...), custom_call_target="tpu_custom_call" | custom-call | tf_op jit(solution)/shard_map/attention/pallas_call | solution.py:540
  90.8 89.1 %take_home.1 = (bf16[256,2048]{1,0:T(8,128)(2,1)}, bf16[256,2048]{1,0:T(8,128)(2,1)}, bf16[256,2048]{1,0:T(8,128)(2,1)}, bf16[256,2048]{1,0:T(8,128)(2,1)}, f32[128,256]{1,0:T(8,128)}) custom-call(bf16[4096,128]{1,0:T(8,128)(2,1)} %get-tuple-element.29.o_ref, bf16[4096,128]{1,0:T(8,128)(2,1)} %get-tuple-element.30.dq_ref, ...), custom_call_target="tpu_custom_call" | custom-call | tf_op jit(solution)/shard_map/take_home/pallas_call | solution.py:398
  180.0 132.2 %hand_over.1 = (bf16[256,2048]{1,0:T(8,128)(2,1)}, bf16[256,2048]{1,0:T(8,128)(2,1)}, bf16[256,2048]{1,0:T(8,128)(2,1)}, bf16[256,2048]{1,0:T(8,128)(2,1)}, f32[128,256]{1,0:T(8,128)}) custom-call(bf16[256,2048]{1,0:T(8,128)(2,1)} %get-tuple-element.35.refs_0_, bf16[256,2048]{1,0:T(8,128)(2,1)} %get-tuple-element.36.refs_1_, ...), custom_call_target="tpu_custom_call" | custom-call | tf_op jit(solution)/shard_map/hand_over/pallas_call | solution.py:567
  (1 shorter events, 0.0 us)
Async XLA Ops:
  0.6 0.9 copy-start

commit v4 on v3

--- a/solution.py
+++ b/solution.py
@@ -10,6 +10,7 @@
 
 HD = 128
 BLOCK = 128
+SIDE = 4
 KMAX = 16
 STEP = 2
 GROUP = 2
@@ -19,6 +20,13 @@
 BF = jnp.bfloat16
 MESH = pl.DeviceIdType.MESH
 NT = (((1,), (1,)), ((), ()))
+SHIFTS = ((1, 0), (0, 1), (3, 0), (0, 3), (1, 1), (3, 3), (1, 3), (3, 1), (2, 1), (1, 2), (2, 3), (3, 2), (2, 0), (0, 2), (2, 2))
+
+
+def shifted(seq, step, back=False):
+    dx, dy = SHIFTS[step]
+    sign = -1 if back else 1
+    return lax.rem(seq // SIDE + SIDE + sign * dx, SIDE) * SIDE + lax.rem(lax.rem(seq, SIDE) + SIDE + sign * dy, SIDE)
 
 
 def columns(index, width):
@@ -128,7 +136,7 @@
 
     def spread(which, step):
         src, dst = tensors[which]
-        other = lax.rem(seq + step, nseq)
+        other = shifted(seq, step)
         return pltpu.make_async_remote_copy(src.at[:, columns(other, HD)], dst.at[columns(seq, mine), :],
                                             a_send.at[which, step], a_recv.at[which, step], device_id=(dp, other), device_id_type=MESH)
 
@@ -144,8 +152,7 @@
     ring.start(0, w_ref)
     ring.start(1, w_ref)
     for which in range(3):
-        @pl.loop(1, nseq)
-        def _(step):
+        for step in range(nseq - 1):
             spread(which, step).start()
         keep(which).start()
     own_m.wait()
@@ -197,8 +204,7 @@
         store(slot).wait()
 
     for which in range(3):
-        @pl.loop(1, nseq)
-        def _(step):
+        for step in range(nseq - 1):
             spread(which, step).wait()
         keep(which).wait()
 
@@ -241,14 +247,20 @@
     z, core = dp // 2, lax.rem(dp, 2)
     mine, width = a_buf.shape[1:]
     rows = width // ndp
+    turns = nseq // 2
+    wide = 2 * HD
     tensors = ((dq_ref, oq_ref), (dk_ref, ok_ref), (dv_ref, ov_ref))
     greet(dp, seq, ndp, nseq)
 
     def slot(offset, other=False):
         return lax.rem(z + chips + offset, chips) * 2 + (1 - core if other else core)
 
-    def head_at(step):
-        return lax.rem(seq + nseq - step, nseq)
+    def pair_at(step):
+        return lax.rem(seq // SIDE + SIDE - lax.rem(step, SIDE), SIDE) * 2 + lax.rem(lax.rem(seq, SIDE) // 2 + step // SIDE, 2)
+
+    def target(step):
+        turn = step // 2
+        return (lax.rem(seq // SIDE + lax.rem(turn, SIDE), SIDE) * 2 + lax.rem(lax.rem(seq, SIDE) // 2 + turn // SIDE, 2)) * 2 + lax.rem(step, 2)
 
     def home(other, source):
         return pltpu.make_async_remote_copy(o_ref.at[columns(other, mine), :], a_buf.at[dp].at[:, columns(source, HD)],
@@ -257,18 +269,18 @@
     def hop(kind, step):
         way = (1, -1, 1 - 2 * lax.rem(step, 2))[kind]
         origin = slot(0) if kind < 2 else slot(-way)
-        piece = a_buf.at[origin].at[:, columns(head_at(step), HD)]
+        piece = a_buf.at[origin].at[:, columns(pair_at(step), wide)]
         return pltpu.make_async_remote_copy(piece, piece, r_send.at[kind, step], r_recv.at[kind, step],
                                             device_id=(slot(way), seq), device_id_type=MESH)
 
     def hand(kind, step):
-        piece = a_buf.at[slot((0, -1, 1, 2)[kind])].at[:, columns(head_at(step), HD)]
+        piece = a_buf.at[slot((0, -1, 1, 2)[kind])].at[:, columns(pair_at(step), wide)]
         return pltpu.make_async_remote_copy(piece, piece, f_send.at[kind, step], f_recv.at[kind, step],
                                             device_id=(slot(0, True), seq), device_id_type=MESH)
 
     def spread(which, step):
         src, dst = tensors[which]
-        other = lax.rem(seq + step, nseq)
+        other = shifted(seq, step)
         return pltpu.make_async_remote_copy(src.at[columns(other, mine), :], dst.at[:, columns(seq, HD)],
                                             g_send.at[which, step], g_recv.at[which, step], device_id=(dp, other), device_id_type=MESH)
 
@@ -287,15 +299,16 @@
     own_out = pltpu.make_async_copy(out_buf, out_ref, local.at[6])
     own_o.start()
 
-    @pl.loop(1, nseq)
+    @pl.loop(0, nseq)
     def _(step):
-        home(lax.rem(seq + step, nseq), seq).start()
+        @pl.when(target(step) != seq)
+        def _():
+            home(target(step), seq).start()
 
     own_c.start()
     own_w.start()
     for which in range(3):
-        @pl.loop(1, nseq)
-        def _(step):
+        for step in range(nseq - 1):
             spread(which, step).start()
         keep(which).start()
 
@@ -304,18 +317,28 @@
         ct_buf[:, source * mine:(source + 1) * mine] = c_buf[source].T
     own_o.wait()
 
-    @pl.loop(0, nseq + 3)
+    def project(tile):
+        at = columns(tile, rows)
+        total = jnp.zeros((mine, rows), jnp.float32)
+        for source in range(ndp):
+            total += jnp.dot(a_buf[dp, :, source * rows:(source + 1) * rows], w_buf[source, :, at], preferred_element_type=jnp.float32)
+        out_buf[:, at] = total.astype(BF)
+
+    @pl.loop(0, turns + 3)
     def _(turn):
-        @pl.when(turn < nseq)
-        def _():
-            @pl.when(turn > 0)
-            def _():
-                home(head_at(turn), head_at(turn)).wait_recv()
+        @pl.when(turn < turns)
+        def _():
+            for side in range(2):
+                head = pair_at(turn) * 2 + side
+
+                @pl.when(head != seq)
+                def _():
+                    home(head, head).wait_recv()
             hop(0, turn).start()
             hop(1, turn).start()
             hand(0, turn).start()
 
-        @pl.when((turn >= 1) & (turn < nseq + 1))
+        @pl.when((turn >= 1) & (turn < turns + 1))
         def _():
             step = turn - 1
             hop(0, step).wait_recv()
@@ -324,38 +347,40 @@
             hand(1, step).start()
             hand(2, step).start()
 
-        @pl.when((turn >= 2) & (turn < nseq + 2))
+        @pl.when((turn >= 2) & (turn < turns + 2))
         def _():
             step = turn - 2
             hop(2, step).wait_recv()
             hand(3, step).start()
 
+        @pl.when(turn == turns - 1)
+        def _():
+            own_w.wait()
+
+        @pl.when((turn >= turns - 1) & (turn < turns + 1))
+        def _():
+            @pl.loop(0, ndp // 2)
+            def _(tile):
+                project((turn - turns + 1) * (ndp // 2) + tile)
+
         @pl.when(turn >= 3)
         def _():
             step = turn - 3
             for kind in range(4):
                 hand(kind, step).wait_recv()
-            at = columns(head_at(step), HD)
-            pieces = a_buf[:, :, at].reshape(ndp * mine, HD)
+            at = columns(pair_at(step), wide)
+            pieces = a_buf[:, :, at].reshape(ndp * mine, wide)
             p_buf[:, at] = jnp.dot(ct_buf[...], pieces, preferred_element_type=jnp.float32).astype(BF)
-
-            @pl.when(step > 0)
-            def _():
-                share(head_at(step), seq).start()
-
-            @pl.when(step == 0)
-            def _():
-                own_p.start()
-
-    own_w.wait()
-
-    @pl.loop(0, ndp)
-    def _(tile):
-        at = columns(tile, rows)
-        total = jnp.zeros((mine, rows), jnp.float32)
-        for source in range(ndp):
-            total += jnp.dot(a_buf[dp, :, source * rows:(source + 1) * rows], w_buf[source, :, at], preferred_element_type=jnp.float32)
-        out_buf[:, at] = total.astype(BF)
+            for side in range(2):
+                head = pair_at(step) * 2 + side
+
+                @pl.when(head != seq)
+                def _():
+                    share(head, seq).start()
+
+                @pl.when(head == seq)
+                def _():
+                    own_p.start()
 
     own_out.start()
     own_p.wait()
@@ -369,17 +394,17 @@
 
     wg_ref[...] = wg_buf[...].T * factor
     for which in range(3):
-        @pl.loop(1, nseq)
-        def _(step):
+        for step in range(nseq - 1):
             spread(which, step).wait()
         keep(which).wait()
 
-    @pl.loop(0, nseq)
+    @pl.loop(1, nseq)
     def _(step):
-        @pl.when(step > 0)
-        def _():
-            home(head_at(step), seq).wait_send()
-            share(head_at(step), seq).wait_send()
+        home(lax.rem(seq + step, nseq), seq).wait_send()
+        share(lax.rem(seq + step, nseq), seq).wait_send()
+
+    @pl.loop(0, turns)
+    def _(step):
         for kind in range(3):
             hop(kind, step).wait_send()
         for kind in range(4):
@@ -404,7 +429,7 @@
             pltpu.VMEM((ndp, mine, width), BF), pltpu.VMEM((ndp, rows, width), BF), pltpu.VMEM((ndp, mine, rows), BF),
             pltpu.VMEM((rows, ndp * mine), BF), pltpu.VMEM((rows, width), BF),
             pltpu.VMEM((nseq, rows, HD), BF), pltpu.VMEM((mine, width), BF), pltpu.VMEM((rows, HD), jnp.float32),
-            dma((nseq,)), dma((nseq,)), dma((3, nseq)), dma((3, nseq)), dma((3, nseq)), dma((3, nseq)), dma((4, nseq)), dma((4, nseq)),
+            dma((nseq,)), dma((nseq,)), dma((3, nseq)), dma((3, nseq)), dma((3, nseq // 2)), dma((3, nseq // 2)), dma((4, nseq // 2)), dma((4, nseq // 2)),
             dma((nseq,)), dma((nseq,)), dma((8,))],
         compiler_params=pltpu.CompilerParams(collective_id=1, has_side_effects=True, vmem_limit_bytes=60 * 2**20),
         name="take_home",
@@ -553,13 +578,17 @@
 
 
 def pass_on(*refs):
-    arrays, sems = refs[:-1], refs[-1]
-    count = len(arrays) // 2
-    copies = [pltpu.make_async_copy(arrays[i], arrays[count + i], sems.at[i]) for i in range(count)]
-    for copy in copies:
-        copy.start()
-    for copy in copies:
-        copy.wait()
+    count = (len(refs) - 1) // 3
+    sources, results, stops, sems = refs[:count], refs[count:2 * count], refs[2 * count:3 * count], refs[-1]
+    fetches = [pltpu.make_async_copy(sources[i], stops[i], sems.at[0, i]) for i in range(count)]
+    stores = [pltpu.make_async_copy(stops[i], results[i], sems.at[1, i]) for i in range(count)]
+    for fetch in fetches:
+        fetch.start()
+    for fetch, store in zip(fetches, stores):
+        fetch.wait()
+        store.start()
+    for store in stores:
+        store.wait()
 
 
 def hand_over(*arrays):
@@ -569,7 +598,7 @@
         out_shape=tuple(jax.ShapeDtypeStruct(x.shape, x.dtype) for x in arrays),
         in_specs=[place] * len(arrays),
         out_specs=(place,) * len(arrays),
-        scratch_shapes=[pltpu.SemaphoreType.DMA((len(arrays),))],
+        scratch_shapes=[pltpu.VMEM(x.shape, x.dtype) for x in arrays] + [pltpu.SemaphoreType.DMA((2, len(arrays)))],
         compiler_params=pltpu.CompilerParams(vmem_limit_bytes=60 * 2**20),
         name="hand_over",
     )(*arrays)

time: 313 us -> 167 us (0.53)
  Pallas kernels: 310 us -> 163 us
    pallas_call x1, Pallas kernels: 132 us -> 3.35 us  [hand_over(): pl.pallas_call(pass_on, out_shape=tuple((jax.ShapeDtypeStruct(x.shape, x....]
    pallas_call x1, Pallas kernels: 89.1 us -> 78.8 us  [take_home(): pl.pallas_call(functools.partial(take, factor), out_shape=(out,) * 4 + (j...]
    pallas_call x1, Pallas kernels: 27.7 us -> 20.2 us  [attention(): pl.pallas_call(attend, out_shape=(out,) * 4, in_specs=[sm, sm, vm, vm, vm...]
where the time goes in v4:
time: 167 us; the launch traced here: 165 us
  Pallas kernels  163 us (98%)
    pallas_call x1, Pallas kernels, take_home(): pl.pallas_call(functools.partial(take, factor), out_shape=(out,) * 4 + (j...  78.8 us
    pallas_call x1, Pallas kernels, bring_in(): pl.pallas_call(bring, out_shape=(head,) * 4 + (jax.ShapeDtypeStruct((ndp,...  60.6 us
    pallas_call x1, Pallas kernels, attention(): pl.pallas_call(attend, out_shape=(out,) * 4, in_specs=[sm, sm, vm, vm, vm...  20.2 us
    pallas_call x1, Pallas kernels, hand_over(): pl.pallas_call(pass_on, out_shape=tuple((jax.ShapeDtypeStruct(x.shape, x....  3.35 us

profile of v4, /device:TPU:1, one launch (start us, length us, event | category | flops | bytes accessed | tf_op | source)
XLA Modules:
  0.0 165.4 jit_solution(14958537870759238174)
XLA Ops:
  0.6 0.0 copy-start
  0.6 0.9 copy-done
  1.5 0.7 copy.13
  2.2 60.6 %bring_in.1 = (bf16[4096,128]{1,0:T(8,128)(2,1)}, bf16[4096,128]{1,0:T(8,128)(2,1)}, bf16[4096,128]{1,0:T(8,128)(2,1)}, bf16[4096,128]{1,0:T(8,128)(2,1)}, bf16[...) custom-call(s32[1,256]{1,0:T(1,128)} %mask_ref.1, bf16[256,2048]{1,0:T(8,128)(2,1)} %bitcast.9, ...), custom_call_target="tpu_custom_call" | custom-call | tf_op jit(solution)/shard_map/bring_in/pallas_call | solution.py:228
  62.9 20.2 %attention.1 = (bf16[4096,128]{1,0:T(8,128)(2,1)}, bf16[4096,128]{1,0:T(8,128)(2,1)}, bf16[4096,128]{1,0:T(8,128)(2,1)}, bf16[4096,128]{1,0:T(8,128)(2,1)}) custom-call(s32[32,16]{1,0:T(8,128)} %bitcast.13, s32[16,32]{1,0:T(8,128)} %live_ref.1, bf16[4096,128]{1,0:T(8,128)(2,1)} %get-tuple-element.25.q_ref, bf16[4096,128]{1,0:T(8,128)(2,1)} %get-tuple-element.26.k_ref, ...), custom_call_target="tpu_custom_call" | custom-call | tf_op jit(solution)/shard_map/attention/pallas_call | solution.py:565
  83.1 78.8 %take_home.1 = (bf16[256,2048]{1,0:T(8,128)(2,1)}, bf16[256,2048]{1,0:T(8,128)(2,1)}, bf16[256,2048]{1,0:T(8,128)(2,1)}, bf16[256,2048]{1,0:T(8,128)(2,1)}, f32[128,256]{1,0:T(8,128)}) custom-call(bf16[4096,128]{1,0:T(8,128)(2,1)} %get-tuple-element.29.o_ref, bf16[4096,128]{1,0:T(8,128)(2,1)} %get-tuple-element.30.dq_ref, ...), custom_call_target="tpu_custom_call" | custom-call | tf_op jit(solution)/shard_map/take_home/pallas_call | solution.py:423
  161.9 3.3 %hand_over.1 = (bf16[256,2048]{1,0:T(8,128)(2,1)}, bf16[256,2048]{1,0:T(8,128)(2,1)}, bf16[256,2048]{1,0:T(8,128)(2,1)}, bf16[256,2048]{1,0:T(8,128)(2,1)}, f32[128,256]{1,0:T(8,128)}) custom-call(bf16[256,2048]{1,0:T(8,128)(2,1)} %get-tuple-element.35.refs_0_, bf16[256,2048]{1,0:T(8,128)(2,1)} %get-tuple-element.36.refs_1_, ...), custom_call_target="tpu_custom_call" | custom-call | tf_op jit(solution)/shard_map/hand_over/pallas_call | solution.py:596
  (1 shorter events, 0.0 us)
Async XLA Ops:
  0.6 0.9 copy-start

commit v5 on v4

--- a/solution.py
+++ b/solution.py
@@ -11,6 +11,7 @@
 HD = 128
 BLOCK = 128
 SIDE = 4
+PIECE = 32
 KMAX = 16
 STEP = 2
 GROUP = 2
@@ -48,9 +49,10 @@
 
 
 class Ring:
-    def __init__(self, part, buf, dp, seq, ndp, send, recv, give, take):
-        self.part, self.buf, self.dp, self.seq = part, buf, dp, seq
+    def __init__(self, shard, buf, dp, seq, ndp, send, recv, give, take):
+        self.shard, self.buf, self.dp, self.seq = shard, buf, dp, seq
         self.chips = ndp // 2
+        self.pieces = shard.shape[0] // PIECE
         self.z, self.core = dp // 2, lax.rem(dp, 2)
         self.send, self.recv, self.give, self.take = send, recv, give, take
 
@@ -58,62 +60,74 @@
         core = 1 - self.core if other else self.core
         return lax.rem(self.z + self.chips + offset, self.chips) * 2 + core
 
-    def half(self, slot, half):
-        return self.part(self.buf.at[slot], half)
-
-    def hop(self, index, source=None):
-        up = index % 2 == 0
-        half = (0, 1, 1, 0, 0, 1)[index]
-        slot = self.slot(0) if index < 4 else self.slot(-1 if up else 1)
-        target = self.slot(1 if up else -1)
-        src = self.half(slot, half) if source is None else self.part(source, half)
-        return pltpu.make_async_remote_copy(src, self.half(slot, half), self.send.at[index], self.recv.at[index],
-                                            device_id=(target, self.seq), device_id_type=MESH)
-
-    def hand(self, index, source=None):
-        if index < 2:
-            slot, half = self.slot(0), index
-        else:
-            slot = self.slot((-1, 1, -1, 1, 2, 2)[index - 2])
-            half = (0, 1, 1, 0, 0, 1)[index - 2]
-        src = self.half(slot, half) if source is None else self.part(source, half)
-        return pltpu.make_async_remote_copy(src, self.half(slot, half), self.give.at[index], self.take.at[index],
+    def piece(self, ref, index):
+        return ref.at[columns(index, PIECE), :]
+
+    def hop(self, kind, index):
+        way = (1, -1, 1 - 2 * lax.rem(index, 2))[kind]
+        origin = self.slot(0) if kind < 2 else self.slot(-way)
+        there = self.piece(self.buf.at[origin], index)
+        return pltpu.make_async_remote_copy(self.piece(self.shard, index) if kind < 2 else there, there,
+                                            self.send.at[kind, index], self.recv.at[kind, index],
+                                            device_id=(self.slot(way), self.seq), device_id_type=MESH)
+
+    def hand(self, kind, index):
+        there = self.piece(self.buf.at[self.slot((0, -1, 1, 2)[kind])], index)
+        return pltpu.make_async_remote_copy(self.piece(self.shard, index) if kind == 0 else there, there,
+                                            self.give.at[kind, index], self.take.at[kind, index],
                                             device_id=(self.slot(0, True), self.seq), device_id_type=MESH)
 
-    def start(self, half, source=None):
-        for index in ((0, 3), (1, 2))[half]:
-            self.hop(index, source).start()
-        self.hand(half, source).start()
+    def start(self):
+        @pl.loop(0, self.pieces)
+        def _(index):
+            self.hop(0, index).start()
+            self.hop(1, index).start()
+
+        @pl.loop(0, self.pieces)
+        def _(index):
+            self.hand(0, index).start()
+
+    def taken(self, *kinds):
+        @pl.loop(0, self.pieces)
+        def _(index):
+            for kind in kinds:
+                self.hand(kind, index).wait_recv()
 
     def run(self, use, late):
         use(self.slot(0))
-        for index in (0, 1):
-            self.hop(index).wait_recv()
-            self.hop(index + 4).start()
-            self.hand(index + 2).start()
-        self.hand(0).wait_recv()
-        self.hand(1).wait_recv()
+        self.taken(0)
         use(self.slot(0, True))
-        for index, offset in ((2, -1), (3, 1)):
-            self.hop(index).wait_recv()
-            self.hand(index + 2).start()
-            use(self.slot(offset))
-        for first, second, offset in ((2, 4, -1), (3, 5, 1)):
-            self.hand(first).wait_recv()
-            self.hand(second).wait_recv()
-            use(self.slot(offset, True))
-        for index in (4, 5):
-            self.hop(index).wait_recv()
-            self.hand(index + 2).start()
+
+        @pl.loop(0, self.pieces)
+        def _(index):
+            self.hop(0, index).wait_recv()
+            self.hop(1, index).wait_recv()
+            self.hop(2, index).start()
+            self.hand(1, index).start()
+            self.hand(2, index).start()
+
+        use(self.slot(-1))
+        use(self.slot(1))
+        self.taken(1, 2)
+        use(self.slot(-1, True))
+        use(self.slot(1, True))
+
+        @pl.loop(0, self.pieces)
+        def _(index):
+            self.hop(2, index).wait_recv()
+            self.hand(3, index).start()
+
         late()
         use(self.slot(2))
-        self.hand(6).wait_recv()
-        self.hand(7).wait_recv()
+        self.taken(3)
         use(self.slot(2, True))
-        for index in range(6):
-            self.hop(index).wait_send()
-        for index in range(8):
-            self.hand(index).wait_send()
+
+        @pl.loop(0, self.pieces)
+        def _(index):
+            for kind in range(3):
+                self.hop(kind, index).wait_send()
+            for kind in range(4):
+                self.hand(kind, index).wait_send()
 
 
 def bring(mask_ref, q_ref, k_ref, v_ref, w_ref, m_ref, hq_ref, hk_ref, hv_ref, hd_ref, wf_ref, mc_ref,
@@ -124,10 +138,7 @@
     tensors = ((q_ref, hq_ref), (k_ref, hk_ref), (v_ref, hv_ref))
     greet(dp, seq, ndp, nseq)
 
-    def row_half(ref, half):
-        return ref.at[pl.ds(half * (rows // 2), rows // 2), :]
-
-    ring = Ring(row_half, w_buf, dp, seq, ndp, w_send, w_recv, f_send, f_recv)
+    ring = Ring(w_ref, w_buf, dp, seq, ndp, w_send, w_recv, f_send, f_recv)
 
     def sides(step):
         other = lax.rem(dp + step, ndp)
@@ -149,8 +160,7 @@
     own_c = pltpu.make_async_copy(m_buf.at[:, columns(dp, rows)], mc_ref.at[dp], local.at[5])
     own_w.start()
     own_m.start()
-    ring.start(0, w_ref)
-    ring.start(1, w_ref)
+    ring.start()
     for which in range(3):
         for step in range(nseq - 1):
             spread(which, step).start()
@@ -222,6 +232,7 @@
     ndp, nseq = lax.axis_size("dp"), lax.axis_size("seq")
     mine, width = q.shape
     rows = w.shape[0]
+    pieces = rows // PIECE
     place = pl.BlockSpec(memory_space=pl.ANY)
     head = jax.ShapeDtypeStruct((mine * nseq, HD), BF)
     dma = pltpu.SemaphoreType.DMA
@@ -232,7 +243,7 @@
         out_specs=(place,) * 6,
         scratch_shapes=[
             pltpu.VMEM((ndp, rows, width), BF), pltpu.VMEM((mine, width), BF), pltpu.VMEM((mine, width), BF),
-            dma((4, nseq)), dma((4, nseq)), dma((6,)), dma((6,)), dma((8,)), dma((8,)), dma((ndp,)), dma((ndp,)), dma((7,)), dma((ndp,))],
+            dma((4, nseq)), dma((4, nseq)), dma((3, pieces)), dma((3, pieces)), dma((4, pieces)), dma((4, pieces)), dma((ndp,)), dma((ndp,)), dma((7,)), dma((ndp,))],
         compiler_params=pltpu.CompilerParams(collective_id=0, has_side_effects=True, vmem_limit_bytes=60 * 2**20),
         name="bring_in",
     )(mask, q, k, v, w, m)
@@ -446,15 +457,16 @@
     def fold(x):
         return x.reshape(-1, 8, x.shape[-1])
 
-    for level in range(levels):
+    for level in range(levels + 1):
         fill_ref[level] = 0
+
     @pl.loop(0, nb)
     def _(b):
-        level = (live_ref[me, b] - 1) // STEP
-        for later in range(1, levels):
-            @pl.when(level < later)
-            def _():
-                fill_ref[later] += 1
+        fill_ref[(live_ref[me, b] - 1) // STEP + 1] += 1
+
+    for level in range(1, levels):
+        fill_ref[level] += fill_ref[level - 1]
+
     @pl.loop(0, nb)
     def _(b):
         level = (live_ref[me, b] - 1) // STEP
@@ -538,7 +550,7 @@
 
     def with_slots(count, turn):
         bs = [order_ref[turn * PAIR + i] for i in range(PAIR)]
-        ats = [[block(pat_ref[b, j]) for j in range(count)] for b in bs]
+        ats = [[block(pat_ref[me, j, b]) for j in range(count)] for b in bs]
         states = [scores(count, b, at, i * KMAX * BLOCK) for i, (b, at) in enumerate(zip(bs, ats))]
         for i, (b, at, state) in enumerate(zip(bs, ats, states)):
             grads(count, b, at, i * KMAX * BLOCK, *state)
@@ -571,7 +583,7 @@
             pltpu.VMEM((length, HD), BF), pltpu.VMEM((length, HD), BF),
             pltpu.VMEM((length, 2 * HD), jnp.float32),
             pltpu.VMEM((PAIR * KMAX * BLOCK, BLOCK), jnp.float32), pltpu.VMEM((PAIR * KMAX * BLOCK, BLOCK), jnp.float32),
-            pltpu.SMEM((length // BLOCK,), jnp.int32), pltpu.SMEM((KMAX // STEP,), jnp.int32)],
+            pltpu.SMEM((length // BLOCK,), jnp.int32), pltpu.SMEM((KMAX // STEP + 1,), jnp.int32)],
         compiler_params=pltpu.CompilerParams(vmem_limit_bytes=60 * 2**20),
         name="attention",
     )(pat, live, q, k, v, d)
@@ -605,8 +617,7 @@
 
 
 def local(queries, keys, values, weight_out, cotangent, hidden_mask, pattern, live_slots):
-    seq = lax.axis_index("seq")
-    pat = lax.dynamic_index_in_dim(pattern, seq, 0, keepdims=False)
+    pat = pattern.transpose(0, 2, 1)
     q, k, v, d, weights, sides = bring_in(hidden_mask, queries[0], keys[0], values[0], weight_out, cotangent[0])
     attn, dq, dk, dv = attention(q, k, v, d, pat, live_slots)
     block_out, dq, dk, dv, weight_grad = hand_over(*take_home(attn, dq, dk, dv, weights, sides))

time: 167 us -> 170 us (1.018)
  Pallas kernels: 163 us -> 167 us
    pallas_call x1, Pallas kernels: 20.2 us -> 29.9 us  [attention(): pl.pallas_call(attend, out_shape=(out,) * 4, in_specs=[sm, sm, vm, vm, vm...]
    pallas_call x1, Pallas kernels: 78.8 us -> 72.7 us  [take_home(): pl.pallas_call(functools.partial(take, factor), out_shape=(out,) * 4 + (j...]
where the time goes in v5:
time: 170 us; the launch traced here: 168 us
  Pallas kernels  167 us (98%)
    pallas_call x1, Pallas kernels, take_home(): pl.pallas_call(functools.partial(take, factor), out_shape=(out,) * 4 + (j...  72.7 us
    pallas_call x1, Pallas kernels, bring_in(): pl.pallas_call(bring, out_shape=(head,) * 4 + (jax.ShapeDtypeStruct((ndp,...  61.1 us
    pallas_call x1, Pallas kernels, attention(): pl.pallas_call(attend, out_shape=(out,) * 4, in_specs=[sm, sm, vm, vm, vm...  29.9 us

profile of v5, /device:TPU:1, one launch (start us, length us, event | category | flops | bytes accessed | tf_op | source)
XLA Modules:
  0.0 167.9 jit_solution(9971303898628717241)
XLA Ops:
  0.6 61.1 %bring_in.1 = (bf16[4096,128]{1,0:T(8,128)(2,1)}, bf16[4096,128]{1,0:T(8,128)(2,1)}, bf16[4096,128]{1,0:T(8,128)(2,1)}, bf16[4096,128]{1,0:T(8,128)(2,1)}, bf16[...) custom-call(s32[1,256]{1,0:T(1,128)} %mask_ref.1, bf16[256,2048]{1,0:T(8,128)(2,1)} %bitcast.9, ...), custom_call_target="tpu_custom_call" | custom-call | tf_op jit(solution)/shard_map/bring_in/pallas_call | solution.py:239
  61.8 29.9 %attention.1 = (bf16[4096,128]{1,0:T(8,128)(2,1)}, bf16[4096,128]{1,0:T(8,128)(2,1)}, bf16[4096,128]{1,0:T(8,128)(2,1)}, bf16[4096,128]{1,0:T(8,128)(2,1)}) custom-call(s32[16,16,32]{2,1,0:T(8,128)} %bitcast.13, s32[16,32]{1,0:T(8,128)} %live_ref.1, bf16[4096,128]{1,0:T(8,128)(2,1)} %get-tuple-element.25.q_ref, bf16[4096,128]{1,0:T(8,128)(2,1)} %get-tuple-element.26.k_ref, ...), custom_call_target="tpu_custom_call" | custom-call | tf_op jit(solution)/shard_map/attention/pallas_call | solution.py:577
  91.7 72.7 %take_home.1 = (bf16[256,2048]{1,0:T(8,128)(2,1)}, bf16[256,2048]{1,0:T(8,128)(2,1)}, bf16[256,2048]{1,0:T(8,128)(2,1)}, bf16[256,2048]{1,0:T(8,128)(2,1)}, f32[128,256]{1,0:T(8,128)}) custom-call(bf16[4096,128]{1,0:T(8,128)(2,1)} %get-tuple-element.29.o_ref, bf16[4096,128]{1,0:T(8,128)(2,1)} %get-tuple-element.30.dq_ref, ...), custom_call_target="tpu_custom_call" | custom-call | tf_op jit(solution)/shard_map/take_home/pallas_call | solution.py:434
  164.4 3.3 %hand_over.1 = (bf16[256,2048]{1,0:T(8,128)(2,1)}, bf16[256,2048]{1,0:T(8,128)(2,1)}, bf16[256,2048]{1,0:T(8,128)(2,1)}, bf16[256,2048]{1,0:T(8,128)(2,1)}, f32[128,256]{1,0:T(8,128)}) custom-call(bf16[256,2048]{1,0:T(8,128)(2,1)} %get-tuple-element.35.refs_0_, bf16[256,2048]{1,0:T(8,128)(2,1)} %get-tuple-element.36.refs_1_, ...), custom_call_target="tpu_custom_call" | custom-call | tf_op jit(solution)/shard_map/hand_over/pallas_call | solution.py:608
